TPU v7x, 32 devices: a whole 2x2x4 slice. The times are simulated.
32 devices in a mesh: groups: 2 (over x), inputs: 16 (over z, y, core).
Axes of the slice: x: 2, y: 2, z: 4, core: 2. Of those that a mesh axis runs over, the one named last changes fastest.
Arguments:
- samples: bfloat16 [128, 548864], P(('groups', 'inputs')), parts along dimension 0, may hold values from -6 to 6
- filter_coefs: float32 [4, 8192], replicated, may hold values from -0.09375 to 0.09375
Outputs:
- visibilities: bfloat16 [4096, 64, 64], P(('groups', 'inputs')), parts along dimension 0
There are 2 independent parts, one for each index of `groups`. A program takes and returns all parts, laid end to end along the dimension named above; an argument that names none is the same for every part. Nothing has to cross between parts.
All inputs are finite; a program needn't handle non-finite values.
Results may differ from a plain program's by a relative error of at most 0.0085.
Values may be sent and summed in bfloat16 or wider, within the bound.
A program may use at most 128 MiB of HBM per device.

v0:
```python
import functools
import math

import jax
import jax.numpy as jnp
import numpy as np
from jax import lax
from jax.experimental import pallas as pl
from jax.experimental.pallas import tpu as pltpu
from jax.sharding import PartitionSpec as P


def phase_table(first, second, period):
    rows = lax.broadcasted_iota(jnp.int32, (first, second), 0)
    cols = lax.broadcasted_iota(jnp.int32, (first, second), 1)
    angle = 2.0 * math.pi / period * (rows * cols % period).astype(jnp.float32)
    return (jnp.cos(angle), -jnp.sin(angle))


def correlate_items(block):
    count = block.shape[0]
    nspec_local = block.shape[2] // 2
    rotated = jnp.concatenate([-block[..., nspec_local:], block[..., :nspec_local]], axis=-1)
    real_sum = jnp.einsum("ikt,jkt->kij", block, block, preferred_element_type=jnp.float32)
    imag_sum = jnp.einsum("ikt,jkt->kij", block, rotated, preferred_element_type=jnp.float32)
    rows = lax.broadcasted_iota(jnp.int32, (count, count), 0)
    cols = lax.broadcasted_iota(jnp.int32, (count, count), 1)
    return (jnp.where(rows >= cols, real_sum, imag_sum) / nspec_local).astype(jnp.bfloat16)


def correlate_turned(block):
    flat_block = block.reshape(block.shape[0], block.shape[2], block.shape[3])
    return correlate_items(flat_block)


def plain_body(samples, filter_coefs):
    in_local, total = samples.shape
    taps_count, nfft_local = filter_coefs.shape
    frame_count = total // nfft_local
    nspec_local = frame_count - taps_count + 1
    width_b = 128
    width_a = nfft_local // width_b
    kept_width = width_b // 4
    frames = samples.reshape(in_local, frame_count, nfft_local).astype(jnp.float32)
    filtered = filter_coefs[0] * frames[:, 0:nspec_local]
    for tap_index in range(1, taps_count):
        filtered = (
            filtered + filter_coefs[tap_index] * frames[:, tap_index : tap_index + nspec_local]
        )
    grid_view = filtered.astype(jnp.bfloat16).reshape(in_local, nspec_local, width_a, width_b)
    first_cos, first_sin = phase_table(width_a, width_a, width_a)
    first_table = jnp.concatenate([first_cos, first_sin], axis=1).astype(jnp.bfloat16)
    first_out = jnp.einsum(
        "itab,ak->itkb", grid_view, first_table, preferred_element_type=jnp.float32
    )
    real_one = first_out[:, :, :width_a]
    imag_one = first_out[:, :, width_a:]
    twist_cos, twist_sin = phase_table(width_a, width_b, nfft_local)
    real_two = real_one * twist_cos - imag_one * twist_sin
    imag_two = real_one * twist_sin + imag_one * twist_cos
    stacked = jnp.concatenate(
        [real_two.astype(jnp.bfloat16), imag_two.astype(jnp.bfloat16)], axis=3
    )
    second_cos, second_sin = phase_table(width_b, width_b, width_b)
    second_cos = second_cos[:, :kept_width]
    second_sin = second_sin[:, :kept_width]
    upper_rows = jnp.concatenate([second_cos, second_sin], axis=1)
    lower_rows = jnp.concatenate([-second_sin, second_cos], axis=1)
    second_table = jnp.concatenate([upper_rows, lower_rows], axis=0).astype(jnp.bfloat16)
    second_out = jnp.einsum(
        "itkn,nq->iqkt", stacked, second_table, preferred_element_type=jnp.float32
    )
    real_out = second_out[:, :kept_width]
    imag_out = second_out[:, kept_width:]
    channels = width_a * kept_width
    spectra = jnp.concatenate(
        [real_out.astype(jnp.bfloat16), imag_out.astype(jnp.bfloat16)], axis=3
    )
    spectra = spectra.reshape(in_local, channels, 2 * nspec_local)
    peers = lax.axis_size("inputs")
    per_peer = channels // peers
    owner_view = spectra.reshape(in_local, peers, per_peer, 2 * nspec_local)
    result = correlate_turned(
        lax.all_to_all(owner_view, "inputs", split_axis=1, concat_axis=0, tiled=True)
    )
    return result


WIDTH_B = 128
BF16 = jnp.bfloat16
F32 = jnp.float32
NT = (((1,), (1,)), ((), ()))


def np_phase(first, second, period):
    turns = np.outer(np.arange(first), np.arange(second)) % period
    angle = np.float32(2.0 * math.pi / period) * turns.astype(np.float32)
    return np.cos(angle), -np.sin(angle)


def make_tables(in_local, width_a, kept):
    nfft = width_a * WIDTH_B
    first = np.concatenate([t.T for t in np_phase(width_a, width_a, width_a)], axis=0)
    first = np.kron(first, np.eye(in_local, dtype=np.float32))
    twist = np.concatenate(
        [np.repeat(t, in_local, axis=0) for t in np_phase(width_a, WIDTH_B, nfft)], axis=0
    )
    cos_b, sin_b = (t[:, :kept].T for t in np_phase(WIDTH_B, WIDTH_B, WIDTH_B))
    second = np.concatenate(
        [np.concatenate([cos_b, -sin_b], axis=1), np.concatenate([sin_b, cos_b], axis=1)], axis=0
    )
    return jnp.asarray(first, BF16), jnp.asarray(twist, F32), jnp.asarray(second, BF16)


def correlator_kernel(
    dims, x_any, coef_any, first_any, twist_any, second_any, order_any, half_ref,
    x_ref, coef_in, first_ref, twist_ref, second_ref, order_ref, coef_ref,
    real_ref, imag_ref, turn_ref, send_ref, recv_ref, vis_ref,
    load_sem, x_sem, send_sem, recv_sem, own_sem,
):
    peers, in_local, nspec, taps, kept, chunks, loads, pad = dims
    rows = first_ref.shape[1]
    width_a = rows // in_local
    pairs = width_a // 2
    step = pairs // chunks
    slot = nspec + pad
    me = lax.axis_index("inputs")

    barrier = pltpu.get_barrier_semaphore()

    def greet(o, carry):
        pl.semaphore_signal(
            barrier, inc=1, device_id={"inputs": lax.rem(me + o, peers)},
            device_id_type=pl.DeviceIdType.MESH,
        )
        return carry

    lax.fori_loop(1, peers, greet, 0)

    t_load = nspec // loads

    def load_frames(n):
        start = 0 if n == 0 else n * t_load + taps - 1
        at = pl.ds(start * rows, ((n + 1) * t_load + taps - 1 - start) * rows)
        return pltpu.make_async_copy(x_any.at[at], x_ref.at[at], x_sem.at[n])

    small = [
        pltpu.make_async_copy(src, dst, load_sem.at[n])
        for n, (src, dst) in enumerate((
            (coef_any, coef_in), (first_any, first_ref), (twist_any, twist_ref),
            (second_any, second_ref), (order_any, order_ref),
        ))
    ]
    small[0].start()
    load_frames(0).start()
    for copy in small[1:]:
        copy.start()
    for n in range(1, loads):
        load_frames(n).start()

    small[0].wait()
    for m in range(taps):
        tap = coef_in[pl.ds(m, width_a, stride=taps), :]
        for i in range(in_local):
            coef_ref[pl.ds(m * rows + i, width_a, stride=in_local), :] = tap
    for copy in small[1:]:
        copy.wait()

    lane_block = 64

    def two_spectra(tp, carry):
        t = tp * 2
        filtered = []
        for r in range(0, rows, lane_block):
            frames = [
                x_ref[pl.ds(pl.multiple_of((t + m) * rows + r, lane_block), lane_block), :].astype(F32)
                for m in range(taps + 1)
            ]
            pair = []
            for late in range(2):
                acc = None
                for m in range(taps):
                    at = m * rows + r
                    term = coef_ref[at:at + lane_block, :] * frames[m + late]
                    acc = term if acc is None else acc + term
                pair.append(acc.astype(BF16))
            filtered.append(jnp.concatenate(pair, axis=1))
        filtered = jnp.concatenate(filtered, axis=0)
        out = jnp.dot(first_ref[...], filtered, preferred_element_type=F32)
        w_re, w_im = twist_ref[:rows, :], twist_ref[rows:, :]
        for late in range(2):
            cols = slice(late * WIDTH_B, (late + 1) * WIDTH_B)
            re, im = out[:rows, cols], out[rows:, cols]
            real_ref[pl.ds(t + late, rows, stride=slot), :] = re * w_re - im * w_im
            imag_ref[pl.ds(t + late, rows, stride=slot), :] = re * w_im + im * w_re
        return carry

    for n in range(loads):
        load_frames(n).wait()
        lax.fori_loop(n * t_load // 2, (n + 1) * t_load // 2, two_spectra, 0, unroll=4)
    pl.semaphore_wait(barrier, peers - 1)

    per_dest = kept // peers * in_local

    def channel_pair(kp, carry):
        parts = []
        for kk in range(2):
            both = []
            for i in range(in_local):
                at = pl.ds(((kp * 2 + kk) * in_local + i) * slot, nspec)
                both.append(jnp.concatenate(
                    [real_ref[at, :].astype(BF16), imag_ref[at, :].astype(BF16)], axis=1
                ))
            both = jnp.concatenate(both, axis=0)
            res = lax.dot_general(second_ref[...], both, NT, preferred_element_type=F32)
            for i in range(in_local):
                cols = slice(i * nspec, (i + 1) * nspec)
                turn_ref[pl.ds(kk * kept * in_local + i, kept, stride=in_local), :] = (
                    jnp.concatenate([res[:kept, cols], res[kept:, cols]], axis=1)
                )
            part = turn_ref[kk * kept * in_local:(kk + 1) * kept * in_local, :]
            parts.append(part.reshape(peers, per_dest, 2 * nspec))
        send_ref[:, kp] = jnp.concatenate(parts, axis=1).astype(BF16)
        return carry

    def remote(c, o):
        dest = lax.rem(me + o, peers)
        at = pl.ds(c * step, step)
        return pltpu.make_async_remote_copy(
            src_ref=send_ref.at[dest, at], dst_ref=recv_ref.at[me, at],
            send_sem=send_sem.at[c, o], recv_sem=recv_sem.at[c, o],
            device_id={"inputs": dest}, device_id_type=pl.DeviceIdType.MESH,
        )

    def chunk(c, carry):
        lax.fori_loop(0, step, lambda n, u: channel_pair(c * step + n, u), 0, unroll=2)

        def push(n, carry):
            remote(c, lax.rem(n + peers // 2 - 1, peers - 1) + 1).start()
            return carry

        lax.fori_loop(0, peers - 1, push, 0)
        return carry

    lax.fori_loop(0, chunks, chunk, 0)
    own = pltpu.make_async_copy(send_ref.at[me], recv_ref.at[me], own_sem)
    own.start()
    own.wait()

    count = peers * in_local
    per = 2 * (kept // peers)
    halves = per // 2
    channels = pairs * per
    i_at = lax.broadcasted_iota(jnp.int32, (count, count), 0)
    j_at = lax.broadcasted_iota(jnp.int32, (count, count), 1)

    def correlate_pair(kp, carry):
        block_rows = recv_ref[:, kp].reshape(per * count, 2 * nspec)
        lined = jnp.dot(order_ref[...], block_rows, preferred_element_type=F32)
        turned = jnp.concatenate([-lined[:, nspec:], lined[:, :nspec]], axis=1).astype(BF16)
        lined = lined.astype(BF16)
        for s in range(per):
            block = lined[s * count:(s + 1) * count]
            rotated = turned[s * count:(s + 1) * count]
            re = lax.dot_general(block, block, NT, preferred_element_type=F32)
            im = lax.dot_general(block, rotated, NT, preferred_element_type=F32)
            vis = jnp.where(i_at >= j_at, re, im) * (1.0 / nspec)
            c = (s % halves) * 2 * pairs + kp * 2 + s // halves
            vis_ref[pl.ds(c, count // 2, stride=channels), :] = jnp.concatenate(
                [vis[:count // 2], vis[count // 2:]], axis=1
            )
        return carry

    def receive(c, carry):
        def arrive(o, carry):
            remote(c, o).wait()
            return carry

        lax.fori_loop(1, peers, arrive, 0)
        lax.fori_loop(0, step, lambda n, u: correlate_pair(c * step + n, u), 0, unroll=2)
        return carry

    lax.fori_loop(0, chunks, receive, 0)
    half_ref[...] = vis_ref[...].astype(BF16)


def turn_kernel(channels, vis_ref, out_ref):
    half = out_ref.shape[0] // 2
    width = out_ref.shape[1]

    def one_row(i, carry):
        block = vis_ref[pl.ds(pl.multiple_of(i * channels, channels), channels), :]
        block = block.astype(F32).T.astype(BF16)
        out_ref[i] = block[:width]
        out_ref[i + half] = block[width:]
        return carry

    lax.fori_loop(0, half, one_row, 0, unroll=4)


def kernel_body(peers, kept, samples, filter_coefs):
    in_local, total = samples.shape
    taps, nfft = filter_coefs.shape
    width_a = nfft // WIDTH_B
    nspec = total // nfft - taps + 1
    rows = width_a * in_local
    pairs = width_a // 2
    chunks = 8
    loads = 4
    pad = 1
    per = 2 * (kept // peers)
    count = peers * in_local
    channels = pairs * per
    x = samples.reshape(in_local, total // WIDTH_B, WIDTH_B).transpose(1, 0, 2)
    x = x.reshape(total // WIDTH_B * in_local, WIDTH_B)
    coefs = filter_coefs.reshape(taps, width_a, WIDTH_B).transpose(1, 0, 2)
    coefs = coefs.reshape(width_a * taps, WIDTH_B)
    first, twist, second = make_tables(in_local, width_a, kept)
    order = np.zeros((per, peers, in_local, peers, per, in_local), np.float32)
    for s in range(per):
        for p in range(peers):
            order[s, p, range(in_local), p, s, range(in_local)] = 1
    order = jnp.asarray(order.reshape(per * count, per * count), BF16)
    blocks = (peers, pairs, per * in_local, 2 * nspec)
    inputs = (x, coefs, first, twist, second, order)
    vis = pl.pallas_call(
        functools.partial(
            correlator_kernel, (peers, in_local, nspec, taps, kept, chunks, loads, pad)
        ),
        out_shape=jax.ShapeDtypeStruct((count // 2 * channels, 2 * count), BF16),
        in_specs=[pl.BlockSpec(memory_space=pl.ANY)] * len(inputs),
        out_specs=pl.BlockSpec(memory_space=pltpu.VMEM),
        scratch_shapes=[pltpu.VMEM(a.shape, a.dtype) for a in inputs] + [
            pltpu.VMEM((taps * rows, WIDTH_B), F32),
            pltpu.VMEM((rows * (nspec + pad), WIDTH_B), F32),
            pltpu.VMEM((rows * (nspec + pad), WIDTH_B), F32),
            pltpu.VMEM((2 * kept * in_local, 2 * nspec), F32),
            pltpu.VMEM(blocks, BF16),
            pltpu.VMEM(blocks, BF16),
            pltpu.VMEM((count // 2 * channels, 2 * count), F32),
            pltpu.SemaphoreType.DMA((len(inputs) - 1,)),
            pltpu.SemaphoreType.DMA((loads,)),
            pltpu.SemaphoreType.DMA((chunks, peers)),
            pltpu.SemaphoreType.DMA((chunks, peers)),
            pltpu.SemaphoreType.DMA,
        ],
        compiler_params=pltpu.CompilerParams(
            collective_id=0, has_side_effects=True, vmem_limit_bytes=56 * 2**20
        ),
        name="correlator",
    )(*inputs)
    out = pl.pallas_call(
        functools.partial(turn_kernel, channels),
        out_shape=jax.ShapeDtypeStruct((count, count, channels), BF16),
        in_specs=[pl.BlockSpec(memory_space=pltpu.VMEM)],
        out_specs=pl.BlockSpec(memory_space=pltpu.VMEM),
        compiler_params=pltpu.CompilerParams(vmem_limit_bytes=32 * 2**20),
        name="turn",
    )(vis)
    return out.transpose(2, 0, 1)


def solution(mesh):
    peers = mesh.shape["inputs"]

    def body(samples, filter_coefs):
        in_local = samples.shape[0]
        kept = WIDTH_B // 4
        whole_q = kept % peers == 0
        if whole_q and (2 * in_local * (kept // peers)) % 16 == 0:
            return kernel_body(peers, kept, samples, filter_coefs)
        return plain_body(samples, filter_coefs)

    return jax.shard_map(
        body,
        mesh=mesh,
        in_specs=(P(("groups", "inputs"), None), P()),
        out_specs=P(("groups", "inputs"), None, None),
        check_vma=False,
    )
```

profile of v0, /device:TPU:0, one launch (start us, length us, event | category | flops | bytes accessed | tf_op | source)
XLA Modules:
  0.0 67.6 jit_solution(2099122519851977059)
XLA Ops:
  0.0 64.5 %correlator.1.vis_ref = bf16[4096,128]{1,0:T(8,128)(2,1)} custom-call(bf16[17152,128]{1,0:T(8,128)(2,1)} %bitcast.11, f32[256,128]{1,0:T(8,128)} %bitcast.12, bf16[512,256]{1,0:T(8,128)(2,1)} %constant.8.clone.first_any, f32[512,128]{1,0:T(8,128)} %constant.9.clone.twist_any, bf16[64,256]{1,0:T(8,128)(2,1)} %constant.10.clone.second_any, ...), custom_call_target="tpu_custom_call" | custom-call | tf_op jit(solution)/shard_map/correlator/pallas_call | solution.py:326
  64.5 0.0 copy-start
  64.6 1.2 %copy-done = bf16[4096,128]{1,0:T(8,128)(2,1)S(1)} copy-done((bf16[4096,128]{1,0:T(8,128)(2,1)S(1)}, bf16[4096,128]{1,0:T(8,128)(2,1)}, u32[]{:S(2)}) %copy-start) | copy-done | bytes 1048600
  65.8 1.8 %turn.1 = bf16[64,64,128]{2,1,0:T(8,128)(2,1)} custom-call(bf16[4096,128]{1,0:T(8,128)(2,1)S(1)} %copy-done), custom_call_target="tpu_custom_call" | custom-call | tf_op jit(solution)/shard_map/turn/pallas_call | solution.py:352
Async XLA Ops:
  64.5 1.2 %copy-start = (bf16[4096,128]{1,0:T(8,128)(2,1)S(1)}, bf16[4096,128]{1,0:T(8,128)(2,1)}, u32[]{:S(2)}) copy-start(bf16[4096,128]{1,0:T(8,128)(2,1)} %correlator.1.vis_ref) | copy-start | bytes 3145732
where the time goes:
time: 67.7 us; the launch traced here: 67.6 us
  Pallas kernels  66.4 us (98%)
  local copies, waits for them, and re-layouts  1.22 us (2%)
    pallas_call x1, Pallas kernels, kernel_body(): pl.pallas_call(functools.partial(correlator_kernel, (peers, in_local, nsp...  64.5 us
    pallas_call x1, Pallas kernels, kernel_body(): pl.pallas_call(functools.partial(turn_kernel, channels), out_shape=jax.Sh...  1.82 us

commit v1 on v0

--- a/solution.py
+++ b/solution.py
@@ -115,34 +115,45 @@
 def correlator_kernel(
     dims, x_any, coef_any, first_any, twist_any, second_any, order_any, half_ref,
     x_ref, coef_in, first_ref, twist_ref, second_ref, order_ref, coef_ref,
-    real_ref, imag_ref, turn_ref, send_ref, recv_ref, vis_ref,
+    real_ref, imag_ref, turn_ref, send_ref, recv_ref, line_ref, quad_ref, vis_ref,
     load_sem, x_sem, send_sem, recv_sem, own_sem,
 ):
-    peers, in_local, nspec, taps, kept, chunks, loads, pad = dims
+    peers, in_local, nspec, taps, kept, span, step, pad = dims
     rows = first_ref.shape[1]
     width_a = rows // in_local
-    pairs = width_a // 2
-    step = pairs // chunks
-    slot = nspec + pad
+    parts = nspec // span
+    shared = WIDTH_B // (2 * span)
+    wide = shared * span
+    groups = width_a // (2 * shared)
+    chunks = parts * groups // step
+    per_part = groups // step
+    slot = span + pad
+    half = peers // 2
     me = lax.axis_index("inputs")
+    side = me // half
+    place = me % half
+
+    def partner(n):
+        near = n // half
+        return ((side + 1 + near) % 2) * half + (place + n % half + near) % half
 
     barrier = pltpu.get_barrier_semaphore()
 
-    def greet(o, carry):
+    def greet(n, carry):
         pl.semaphore_signal(
-            barrier, inc=1, device_id={"inputs": lax.rem(me + o, peers)},
+            barrier, inc=1, device_id={"inputs": partner(n)},
             device_id_type=pl.DeviceIdType.MESH,
         )
         return carry
 
-    lax.fori_loop(1, peers, greet, 0)
-
-    t_load = nspec // loads
-
-    def load_frames(n):
-        start = 0 if n == 0 else n * t_load + taps - 1
-        at = pl.ds(start * rows, ((n + 1) * t_load + taps - 1 - start) * rows)
+    lax.fori_loop(0, peers - 1, greet, 0)
+
+    def load_frames(start, count, n):
+        at = pl.ds(start * rows, count * rows)
         return pltpu.make_async_copy(x_any.at[at], x_ref.at[at], x_sem.at[n])
+
+    def load_part(h):
+        return load_frames(h * span + taps - 1, span, h)
 
     small = [
         pltpu.make_async_copy(src, dst, load_sem.at[n])
@@ -152,11 +163,12 @@
         ))
     ]
     small[0].start()
-    load_frames(0).start()
+    load_frames(0, taps - 1, parts).start()
+    load_part(0).start()
     for copy in small[1:]:
         copy.start()
-    for n in range(1, loads):
-        load_frames(n).start()
+    for n in range(1, parts):
+        load_part(n).start()
 
     small[0].wait()
     for m in range(taps):
@@ -165,11 +177,13 @@
             coef_ref[pl.ds(m * rows + i, width_a, stride=in_local), :] = tap
     for copy in small[1:]:
         copy.wait()
+    load_frames(0, taps - 1, parts).wait()
 
     lane_block = 64
 
-    def two_spectra(tp, carry):
-        t = tp * 2
+    def two_spectra(h, tp):
+        late_t = tp * 2
+        t = h * span + late_t
         filtered = []
         for r in range(0, rows, lane_block):
             frames = [
@@ -191,58 +205,73 @@
         for late in range(2):
             cols = slice(late * WIDTH_B, (late + 1) * WIDTH_B)
             re, im = out[:rows, cols], out[rows:, cols]
-            real_ref[pl.ds(t + late, rows, stride=slot), :] = re * w_re - im * w_im
-            imag_ref[pl.ds(t + late, rows, stride=slot), :] = re * w_im + im * w_re
-        return carry
-
-    for n in range(loads):
-        load_frames(n).wait()
-        lax.fori_loop(n * t_load // 2, (n + 1) * t_load // 2, two_spectra, 0, unroll=4)
-    pl.semaphore_wait(barrier, peers - 1)
+            real_ref[pl.ds(late_t + late, rows, stride=slot), :] = re * w_re - im * w_im
+            imag_ref[pl.ds(late_t + late, rows, stride=slot), :] = re * w_im + im * w_re
 
     per_dest = kept // peers * in_local
 
-    def channel_pair(kp, carry):
-        parts = []
+    def channel_group(h, kp):
+        parts_out = []
         for kk in range(2):
             both = []
             for i in range(in_local):
-                at = pl.ds(((kp * 2 + kk) * in_local + i) * slot, nspec)
-                both.append(jnp.concatenate(
-                    [real_ref[at, :].astype(BF16), imag_ref[at, :].astype(BF16)], axis=1
-                ))
+                for u in range(shared):
+                    k = (kp * 2 + kk) * shared + u
+                    at = pl.ds((k * in_local + i) * slot, span)
+                    both.append(jnp.concatenate(
+                        [real_ref[at, :].astype(BF16), imag_ref[at, :].astype(BF16)], axis=1
+                    ))
             both = jnp.concatenate(both, axis=0)
             res = lax.dot_general(second_ref[...], both, NT, preferred_element_type=F32)
             for i in range(in_local):
-                cols = slice(i * nspec, (i + 1) * nspec)
+                cols = slice(i * wide, (i + 1) * wide)
                 turn_ref[pl.ds(kk * kept * in_local + i, kept, stride=in_local), :] = (
                     jnp.concatenate([res[:kept, cols], res[kept:, cols]], axis=1)
                 )
             part = turn_ref[kk * kept * in_local:(kk + 1) * kept * in_local, :]
-            parts.append(part.reshape(peers, per_dest, 2 * nspec))
-        send_ref[:, kp] = jnp.concatenate(parts, axis=1).astype(BF16)
-        return carry
-
-    def remote(c, o):
-        dest = lax.rem(me + o, peers)
+            parts_out.append(part.reshape(peers, per_dest, WIDTH_B))
+        send_ref[:, h * groups + kp] = jnp.concatenate(parts_out, axis=1).astype(BF16)
+
+    def remote(c, n):
+        dest = partner(n)
         at = pl.ds(c * step, step)
         return pltpu.make_async_remote_copy(
             src_ref=send_ref.at[dest, at], dst_ref=recv_ref.at[me, at],
-            send_sem=send_sem.at[c, o], recv_sem=recv_sem.at[c, o],
+            send_sem=send_sem.at[c, n], recv_sem=recv_sem.at[c, n],
             device_id={"inputs": dest}, device_id_type=pl.DeviceIdType.MESH,
         )
 
-    def chunk(c, carry):
-        lax.fori_loop(0, step, lambda n, u: channel_pair(c * step + n, u), 0, unroll=2)
-
-        def push(n, carry):
-            remote(c, lax.rem(n + peers // 2 - 1, peers - 1) + 1).start()
-            return carry
-
-        lax.fori_loop(0, peers - 1, push, 0)
+    def forward(h, carry):
+        load_part(h).wait()
+
+        def spectra(tp, u):
+            two_spectra(h, tp)
+            return u
+
+        lax.fori_loop(0, span // 2, spectra, 0, unroll=4)
+
+        @pl.when(h == 0)
+        def _():
+            pl.semaphore_wait(barrier, peers - 1)
+
+        def send_chunk(c, u):
+            def one(n, v):
+                channel_group(h, c * step + n)
+                return v
+
+            lax.fori_loop(0, step, one, 0, unroll=2)
+
+            def push(n, v):
+                remote(h * per_part + c, n).start()
+                return v
+
+            lax.fori_loop(0, peers - 1, push, 0)
+            return u
+
+        lax.fori_loop(0, per_part, send_chunk, 0)
         return carry
 
-    lax.fori_loop(0, chunks, chunk, 0)
+    lax.fori_loop(0, parts, forward, 0)
     own = pltpu.make_async_copy(send_ref.at[me], recv_ref.at[me], own_sem)
     own.start()
     own.wait()
@@ -250,37 +279,78 @@
     count = peers * in_local
     per = 2 * (kept // peers)
     halves = per // 2
-    channels = pairs * per
-    i_at = lax.broadcasted_iota(jnp.int32, (count, count), 0)
-    j_at = lax.broadcasted_iota(jnp.int32, (count, count), 1)
-
-    def correlate_pair(kp, carry):
-        block_rows = recv_ref[:, kp].reshape(per * count, 2 * nspec)
-        lined = jnp.dot(order_ref[...], block_rows, preferred_element_type=F32)
-        turned = jnp.concatenate([-lined[:, nspec:], lined[:, :nspec]], axis=1).astype(BF16)
-        lined = lined.astype(BF16)
+    channels = width_a * halves
+    low = count // 2
+    i_at = lax.broadcasted_iota(jnp.int32, (low, WIDTH_B), 0)
+    lane = lax.broadcasted_iota(jnp.int32, (low, WIDTH_B), 1)
+    first_half = lane < count
+    top_real = i_at >= lane
+    low_real = i_at + low >= lane - count
+    lane_row = lax.broadcasted_iota(jnp.int32, (count, WIDTH_B), 1)
+    masks = [
+        jnp.where((lane_row % wide) // span == u, 1.0, 0.0).astype(BF16) for u in range(shared)
+    ]
+
+    def swap(v):
+        return jnp.concatenate([v[:, wide:], v[:, :wide]], axis=1)
+
+    def line_up(g):
+        lined = jnp.dot(
+            order_ref[...], recv_ref[:, g].reshape(per * count, WIDTH_B),
+            preferred_element_type=F32,
+        )
+        line_ref[g] = lined.astype(BF16)
+        quad_ref[g] = jnp.concatenate([-lined[:, wide:], lined[:, :wide]], axis=1).astype(BF16)
+
+    def correlate(kp):
         for s in range(per):
-            block = lined[s * count:(s + 1) * count]
-            rotated = turned[s * count:(s + 1) * count]
-            re = lax.dot_general(block, block, NT, preferred_element_type=F32)
-            im = lax.dot_general(block, rotated, NT, preferred_element_type=F32)
-            vis = jnp.where(i_at >= j_at, re, im) * (1.0 / nspec)
-            c = (s % halves) * 2 * pairs + kp * 2 + s // halves
-            vis_ref[pl.ds(c, count // 2, stride=channels), :] = jnp.concatenate(
-                [vis[:count // 2], vis[count // 2:]], axis=1
+            at = slice(s * count, (s + 1) * count)
+            tiles = [line_ref[h * groups + kp, at, :] for h in range(parts)]
+            turned = [quad_ref[h * groups + kp, at, :] for h in range(parts)]
+            right = jnp.concatenate(
+                [jnp.concatenate(tiles, axis=1), jnp.concatenate(turned, axis=1)], axis=0
             )
+            left = jnp.concatenate(
+                [jnp.concatenate([t * m for t in tiles], axis=1) for m in masks], axis=0
+            )
+            res = lax.dot_general(left, right, NT, preferred_element_type=F32)
+            for u in range(shared):
+                top = res[u * count:u * count + low]
+                bottom = res[u * count + low:(u + 1) * count]
+                vis = jnp.where(
+                    first_half,
+                    jnp.where(top_real, top, swap(top)),
+                    jnp.where(low_real, swap(bottom), bottom),
+                )
+                c = (s % halves) * width_a + (kp * 2 + s // halves) * shared + u
+                vis_ref[pl.ds(c, low, stride=channels), :] = vis * (1.0 / nspec)
+
+    def receive(c, carry):
+        def arrive(n, u):
+            remote(c, n).wait()
+            return u
+
+        lax.fori_loop(0, peers - 1, arrive, 0)
+
+        def one(n, u):
+            line_up(c * step + n)
+            return u
+
+        lax.fori_loop(0, step, one, 0, unroll=2)
         return carry
 
-    def receive(c, carry):
-        def arrive(o, carry):
-            remote(c, o).wait()
-            return carry
-
-        lax.fori_loop(1, peers, arrive, 0)
-        lax.fori_loop(0, step, lambda n, u: correlate_pair(c * step + n, u), 0, unroll=2)
+    def finish(c, carry):
+        receive((parts - 1) * per_part + c, 0)
+
+        def one(n, u):
+            correlate(c * step + n)
+            return u
+
+        lax.fori_loop(0, step, one, 0)
         return carry
 
-    lax.fori_loop(0, chunks, receive, 0)
+    lax.fori_loop(0, (parts - 1) * per_part, receive, 0)
+    lax.fori_loop(0, per_part, finish, 0)
     half_ref[...] = vis_ref[...].astype(BF16)
 
 
@@ -304,13 +374,15 @@
     width_a = nfft // WIDTH_B
     nspec = total // nfft - taps + 1
     rows = width_a * in_local
-    pairs = width_a // 2
-    chunks = 8
-    loads = 4
+    span = 16
+    step = 4
     pad = 1
+    parts = nspec // span
+    groups = width_a * span // WIDTH_B
+    chunks = parts * groups // step
     per = 2 * (kept // peers)
     count = peers * in_local
-    channels = pairs * per
+    channels = width_a * per // 2
     x = samples.reshape(in_local, total // WIDTH_B, WIDTH_B).transpose(1, 0, 2)
     x = x.reshape(total // WIDTH_B * in_local, WIDTH_B)
     coefs = filter_coefs.reshape(taps, width_a, WIDTH_B).transpose(1, 0, 2)
@@ -321,25 +393,28 @@
         for p in range(peers):
             order[s, p, range(in_local), p, s, range(in_local)] = 1
     order = jnp.asarray(order.reshape(per * count, per * count), BF16)
-    blocks = (peers, pairs, per * in_local, 2 * nspec)
+    blocks = (peers, parts * groups, per * in_local, WIDTH_B)
+    lines = (parts * groups, per * count, WIDTH_B)
     inputs = (x, coefs, first, twist, second, order)
     vis = pl.pallas_call(
         functools.partial(
-            correlator_kernel, (peers, in_local, nspec, taps, kept, chunks, loads, pad)
+            correlator_kernel, (peers, in_local, nspec, taps, kept, span, step, pad)
         ),
         out_shape=jax.ShapeDtypeStruct((count // 2 * channels, 2 * count), BF16),
         in_specs=[pl.BlockSpec(memory_space=pl.ANY)] * len(inputs),
         out_specs=pl.BlockSpec(memory_space=pltpu.VMEM),
         scratch_shapes=[pltpu.VMEM(a.shape, a.dtype) for a in inputs] + [
             pltpu.VMEM((taps * rows, WIDTH_B), F32),
-            pltpu.VMEM((rows * (nspec + pad), WIDTH_B), F32),
-            pltpu.VMEM((rows * (nspec + pad), WIDTH_B), F32),
-            pltpu.VMEM((2 * kept * in_local, 2 * nspec), F32),
+            pltpu.VMEM((rows * (span + pad), WIDTH_B), F32),
+            pltpu.VMEM((rows * (span + pad), WIDTH_B), F32),
+            pltpu.VMEM((2 * kept * in_local, WIDTH_B), F32),
             pltpu.VMEM(blocks, BF16),
             pltpu.VMEM(blocks, BF16),
+            pltpu.VMEM(lines, BF16),
+            pltpu.VMEM(lines, BF16),
             pltpu.VMEM((count // 2 * channels, 2 * count), F32),
             pltpu.SemaphoreType.DMA((len(inputs) - 1,)),
-            pltpu.SemaphoreType.DMA((loads,)),
+            pltpu.SemaphoreType.DMA((parts + 1,)),
             pltpu.SemaphoreType.DMA((chunks, peers)),
             pltpu.SemaphoreType.DMA((chunks, peers)),
             pltpu.SemaphoreType.DMA,
@@ -366,8 +441,11 @@
     def body(samples, filter_coefs):
         in_local = samples.shape[0]
         kept = WIDTH_B // 4
-        whole_q = kept % peers == 0
-        if whole_q and (2 * in_local * (kept // peers)) % 16 == 0:
+        nfft = filter_coefs.shape[1]
+        nspec = samples.shape[1] // nfft - filter_coefs.shape[0] + 1
+        fits = kept % peers == 0 and peers % 2 == 0 and 2 * peers * in_local == WIDTH_B
+        fits = fits and nspec % 16 == 0 and nfft % (32 * WIDTH_B) == 0
+        if fits and (2 * in_local * (kept // peers)) % 16 == 0:
             return kernel_body(peers, kept, samples, filter_coefs)
         return plain_body(samples, filter_coefs)
 

time: 67.7 us -> 66.2 us (0.978)
  Pallas kernels: 66.4 us -> 64.8 us
    pallas_call x1, Pallas kernels: 64.5 us -> 63 us  [kernel_body(): pl.pallas_call(functools.partial(correlator_kernel, (peers, in_local, nsp...]
where the time goes in v1:
time: 66.2 us; the launch traced here: 66.1 us
  Pallas kernels  64.8 us (98%)
  local copies, waits for them, and re-layouts  1.22 us (2%)
    pallas_call x1, Pallas kernels, kernel_body(): pl.pallas_call(functools.partial(correlator_kernel, (peers, in_local, nsp...  63 us
    pallas_call x1, Pallas kernels, kernel_body(): pl.pallas_call(functools.partial(turn_kernel, channels), out_shape=jax.Sh...  1.82 us

profile of v1, /device:TPU:0, one launch (start us, length us, event | category | flops | bytes accessed | tf_op | source)
XLA Modules:
  0.0 66.1 jit_solution(7057166369772495983)
XLA Ops:
  0.0 63.0 %correlator.1.vis_ref = bf16[4096,128]{1,0:T(8,128)(2,1)} custom-call(bf16[17152,128]{1,0:T(8,128)(2,1)} %bitcast.11, f32[256,128]{1,0:T(8,128)} %bitcast.12, bf16[512,256]{1,0:T(8,128)(2,1)} %constant.8.clone.first_any, f32[512,128]{1,0:T(8,128)} %constant.9.clone.twist_any, bf16[64,256]{1,0:T(8,128)(2,1)} %constant.10.clone.second_any, ...), custom_call_target="tpu_custom_call" | custom-call | tf_op jit(solution)/shard_map/correlator/pallas_call | solution.py:399
  63.0 0.0 copy-start
  63.0 1.2 %copy-done = bf16[4096,128]{1,0:T(8,128)(2,1)S(1)} copy-done((bf16[4096,128]{1,0:T(8,128)(2,1)S(1)}, bf16[4096,128]{1,0:T(8,128)(2,1)}, u32[]{:S(2)}) %copy-start) | copy-done | bytes 1048600
  64.2 1.8 %turn.1 = bf16[64,64,128]{2,1,0:T(8,128)(2,1)} custom-call(bf16[4096,128]{1,0:T(8,128)(2,1)S(1)} %copy-done), custom_call_target="tpu_custom_call" | custom-call | tf_op jit(solution)/shard_map/turn/pallas_call | solution.py:427
Async XLA Ops:
  63.0 1.2 %copy-start = (bf16[4096,128]{1,0:T(8,128)(2,1)S(1)}, bf16[4096,128]{1,0:T(8,128)(2,1)}, u32[]{:S(2)}) copy-start(bf16[4096,128]{1,0:T(8,128)(2,1)} %correlator.1.vis_ref) | copy-start | bytes 3145732

commit v2 on v1

--- a/solution.py
+++ b/solution.py
@@ -115,7 +115,7 @@
 def correlator_kernel(
     dims, x_any, coef_any, first_any, twist_any, second_any, order_any, half_ref,
     x_ref, coef_in, first_ref, twist_ref, second_ref, order_ref, coef_ref,
-    real_ref, imag_ref, turn_ref, send_ref, recv_ref, line_ref, quad_ref, vis_ref,
+    real_ref, imag_ref, turn_ref, send_ref, recv_ref, line_ref, quad_ref, sum_ref, vis_ref,
     load_sem, x_sem, send_sem, recv_sem, own_sem,
 ):
     peers, in_local, nspec, taps, kept, span, step, pad = dims
@@ -125,17 +125,11 @@
     shared = WIDTH_B // (2 * span)
     wide = shared * span
     groups = width_a // (2 * shared)
-    chunks = parts * groups // step
-    per_part = groups // step
     slot = span + pad
-    half = peers // 2
     me = lax.axis_index("inputs")
-    side = me // half
-    place = me % half
 
     def partner(n):
-        near = n // half
-        return ((side + 1 + near) % 2) * half + (place + n % half + near) % half
+        return lax.rem(me + n + 1, peers)
 
     barrier = pltpu.get_barrier_semaphore()
 
@@ -232,15 +226,22 @@
             parts_out.append(part.reshape(peers, per_dest, WIDTH_B))
         send_ref[:, h * groups + kp] = jnp.concatenate(parts_out, axis=1).astype(BF16)
 
-    def remote(c, n):
+    def remote(c, size, n):
         dest = partner(n)
-        at = pl.ds(c * step, step)
+        at = pl.ds((c + 1) * step - size, size)
         return pltpu.make_async_remote_copy(
             src_ref=send_ref.at[dest, at], dst_ref=recv_ref.at[me, at],
             send_sem=send_sem.at[c, n], recv_sem=recv_sem.at[c, n],
             device_id={"inputs": dest}, device_id_type=pl.DeviceIdType.MESH,
         )
 
+    def push(c, size):
+        def one(n, u):
+            remote(c, size, n).start()
+            return u
+
+        lax.fori_loop(0, peers - 1, one, 0)
+
     def forward(h, carry):
         load_part(h).wait()
 
@@ -260,15 +261,19 @@
                 return v
 
             lax.fori_loop(0, step, one, 0, unroll=2)
-
-            def push(n, v):
-                remote(h * per_part + c, n).start()
-                return v
-
-            lax.fori_loop(0, peers - 1, push, 0)
+            split = (h == 0) | (h == parts - 1)
+
+            @pl.when(split)
+            def _():
+                push(2 * h + c, step)
+
+            @pl.when(jnp.logical_not(split) & (c == 1))
+            def _():
+                push(2 * h + c, groups)
+
             return u
 
-        lax.fori_loop(0, per_part, send_chunk, 0)
+        lax.fori_loop(0, 2, send_chunk, 0)
         return carry
 
     lax.fori_loop(0, parts, forward, 0)
@@ -291,8 +296,12 @@
         jnp.where((lane_row % wide) // span == u, 1.0, 0.0).astype(BF16) for u in range(shared)
     ]
 
+    signs = jnp.where(
+        lax.broadcasted_iota(jnp.int32, (per * count, WIDTH_B), 1) < wide, -1.0, 1.0
+    )
+
     def swap(v):
-        return jnp.concatenate([v[:, wide:], v[:, :wide]], axis=1)
+        return pltpu.roll(v, wide, 1)
 
     def line_up(g):
         lined = jnp.dot(
@@ -300,20 +309,28 @@
             preferred_element_type=F32,
         )
         line_ref[g] = lined.astype(BF16)
-        quad_ref[g] = jnp.concatenate([-lined[:, wide:], lined[:, :wide]], axis=1).astype(BF16)
+        quad_ref[g] = (swap(lined) * signs).astype(BF16)
+
+    def gram(kp, s, first, last):
+        at = slice(s * count, (s + 1) * count)
+        tiles = [line_ref[h * groups + kp, at, :] for h in range(first, last)]
+        turned = [quad_ref[h * groups + kp, at, :] for h in range(first, last)]
+        right = jnp.concatenate(
+            [jnp.concatenate(tiles, axis=1), jnp.concatenate(turned, axis=1)], axis=0
+        )
+        left = jnp.concatenate(
+            [jnp.concatenate([t * m for t in tiles], axis=1) for m in masks], axis=0
+        )
+        return lax.dot_general(left, right, NT, preferred_element_type=F32)
+
+    def correlate_early(kp, u):
+        for s in range(per):
+            sum_ref[kp * per + s] = gram(kp, s, 0, parts - 2)
+        return u
 
     def correlate(kp):
         for s in range(per):
-            at = slice(s * count, (s + 1) * count)
-            tiles = [line_ref[h * groups + kp, at, :] for h in range(parts)]
-            turned = [quad_ref[h * groups + kp, at, :] for h in range(parts)]
-            right = jnp.concatenate(
-                [jnp.concatenate(tiles, axis=1), jnp.concatenate(turned, axis=1)], axis=0
-            )
-            left = jnp.concatenate(
-                [jnp.concatenate([t * m for t in tiles], axis=1) for m in masks], axis=0
-            )
-            res = lax.dot_general(left, right, NT, preferred_element_type=F32)
+            res = sum_ref[kp * per + s] + gram(kp, s, parts - 2, parts)
             for u in range(shared):
                 top = res[u * count:u * count + low]
                 bottom = res[u * count + low:(u + 1) * count]
@@ -325,47 +342,83 @@
                 c = (s % halves) * width_a + (kp * 2 + s // halves) * shared + u
                 vis_ref[pl.ds(c, low, stride=channels), :] = vis * (1.0 / nspec)
 
-    def receive(c, carry):
-        def arrive(n, u):
-            remote(c, n).wait()
+    def arrive(c, size):
+        def one(n, u):
+            remote(c, size, n).wait()
             return u
 
-        lax.fori_loop(0, peers - 1, arrive, 0)
-
+        lax.fori_loop(0, peers - 1, one, 0)
+
+    def lines(h):
         def one(n, u):
-            line_up(c * step + n)
+            line_up(h * groups + n)
             return u
 
-        lax.fori_loop(0, step, one, 0, unroll=2)
+        lax.fori_loop(0, groups, one, 0, unroll=2)
+
+    def middle(h, carry):
+        arrive(2 * h + 1, groups)
+        lines(h)
+
+        @pl.when(h == parts - 3)
+        def _():
+            lax.fori_loop(0, groups, correlate_early, 0)
+
         return carry
 
     def finish(c, carry):
-        receive((parts - 1) * per_part + c, 0)
+        arrive(2 * (parts - 1) + c, step)
 
         def one(n, u):
-            correlate(c * step + n)
+            kp = c * step + n
+            line_up((parts - 1) * groups + kp)
+            correlate(kp)
             return u
 
         lax.fori_loop(0, step, one, 0)
         return carry
 
-    lax.fori_loop(0, (parts - 1) * per_part, receive, 0)
-    lax.fori_loop(0, per_part, finish, 0)
+    arrive(0, step)
+    arrive(1, step)
+    lines(0)
+    lax.fori_loop(1, parts - 1, middle, 0)
+    lax.fori_loop(0, 2, finish, 0)
     half_ref[...] = vis_ref[...].astype(BF16)
 
 
-def turn_kernel(channels, vis_ref, out_ref):
+def turn_kernel(channels, pieces, vis_any, out_any, vis_ref, out_ref, in_sem, out_sem):
     half = out_ref.shape[0] // 2
     width = out_ref.shape[1]
-
-    def one_row(i, carry):
-        block = vis_ref[pl.ds(pl.multiple_of(i * channels, channels), channels), :]
-        block = block.astype(F32).T.astype(BF16)
-        out_ref[i] = block[:width]
-        out_ref[i + half] = block[width:]
-        return carry
-
-    lax.fori_loop(0, half, one_row, 0, unroll=4)
+    each = half // pieces
+
+    def fetch(p):
+        at = pl.ds(p * each * channels, each * channels)
+        return pltpu.make_async_copy(vis_any.at[at], vis_ref.at[at], in_sem.at[p])
+
+    def put(p, upper):
+        at = pl.ds(p * each + upper * half, each)
+        return pltpu.make_async_copy(out_ref.at[at], out_any.at[at], out_sem.at[upper, p])
+
+    for p in range(pieces):
+        fetch(p).start()
+
+    for p in range(pieces):
+        fetch(p).wait()
+
+        def one_row(n, carry):
+            i = p * each + n
+            block = vis_ref[pl.ds(pl.multiple_of(i * channels, channels), channels), :]
+            block = block.astype(F32).T.astype(BF16)
+            out_ref[i] = block[:width]
+            out_ref[i + half] = block[width:]
+            return carry
+
+        lax.fori_loop(0, each, one_row, 0, unroll=4)
+        put(p, 0).start()
+        put(p, 1).start()
+    for p in range(pieces):
+        put(p, 0).wait()
+        put(p, 1).wait()
 
 
 def kernel_body(peers, kept, samples, filter_coefs):
@@ -375,11 +428,12 @@
     nspec = total // nfft - taps + 1
     rows = width_a * in_local
     span = 16
-    step = 4
+    pieces = 4
     pad = 1
     parts = nspec // span
     groups = width_a * span // WIDTH_B
-    chunks = parts * groups // step
+    step = groups // 2
+    chunks = 2 * parts
     per = 2 * (kept // peers)
     count = peers * in_local
     channels = width_a * per // 2
@@ -412,6 +466,7 @@
             pltpu.VMEM(blocks, BF16),
             pltpu.VMEM(lines, BF16),
             pltpu.VMEM(lines, BF16),
+            pltpu.VMEM((groups * per, per * count, WIDTH_B), F32),
             pltpu.VMEM((count // 2 * channels, 2 * count), F32),
             pltpu.SemaphoreType.DMA((len(inputs) - 1,)),
             pltpu.SemaphoreType.DMA((parts + 1,)),
@@ -425,10 +480,16 @@
         name="correlator",
     )(*inputs)
     out = pl.pallas_call(
-        functools.partial(turn_kernel, channels),
+        functools.partial(turn_kernel, channels, pieces),
         out_shape=jax.ShapeDtypeStruct((count, count, channels), BF16),
-        in_specs=[pl.BlockSpec(memory_space=pltpu.VMEM)],
-        out_specs=pl.BlockSpec(memory_space=pltpu.VMEM),
+        in_specs=[pl.BlockSpec(memory_space=pltpu.HBM)],
+        out_specs=pl.BlockSpec(memory_space=pl.ANY),
+        scratch_shapes=[
+            pltpu.VMEM((count // 2 * channels, 2 * count), BF16),
+            pltpu.VMEM((count, count, channels), BF16),
+            pltpu.SemaphoreType.DMA((pieces,)),
+            pltpu.SemaphoreType.DMA((2, pieces)),
+        ],
         compiler_params=pltpu.CompilerParams(vmem_limit_bytes=32 * 2**20),
         name="turn",
     )(vis)
@@ -443,8 +504,8 @@
         kept = WIDTH_B // 4
         nfft = filter_coefs.shape[1]
         nspec = samples.shape[1] // nfft - filter_coefs.shape[0] + 1
-        fits = kept % peers == 0 and peers % 2 == 0 and 2 * peers * in_local == WIDTH_B
-        fits = fits and nspec % 16 == 0 and nfft % (32 * WIDTH_B) == 0
+        fits = kept % peers == 0 and 2 * peers * in_local == WIDTH_B
+        fits = fits and nspec % 16 == 0 and nspec >= 64 and nfft % (32 * WIDTH_B) == 0
         if fits and (2 * in_local * (kept // peers)) % 16 == 0:
             return kernel_body(peers, kept, samples, filter_coefs)
         return plain_body(samples, filter_coefs)

time: 66.2 us -> 63.5 us (0.959)
  Pallas kernels: 64.8 us -> 62.1 us
    pallas_call x1, Pallas kernels: 63 us -> 60.3 us  [kernel_body(): pl.pallas_call(functools.partial(correlator_kernel, (peers, in_local, nsp...]
where the time goes in v2:
time: 63.5 us; the launch traced here: 63.3 us
  Pallas kernels  62.1 us (98%)
  local copies, waits for them, and re-layouts  1.22 us (2%)
    pallas_call x1, Pallas kernels, kernel_body(): pl.pallas_call(functools.partial(correlator_kernel, (peers, in_local, nsp...  60.3 us
    pallas_call x1, Pallas kernels, kernel_body(): pl.pallas_call(functools.partial(turn_kernel, channels, pieces), out_shap...  1.74 us

profile of v2, /device:TPU:0, one launch (start us, length us, event | category | flops | bytes accessed | tf_op | source)
XLA Modules:
  0.0 63.3 jit_solution(1062334884021170680)
XLA Ops:
  0.0 60.3 %correlator.1.vis_any = bf16[4096,128]{1,0:T(8,128)(2,1)} custom-call(bf16[17152,128]{1,0:T(8,128)(2,1)} %bitcast.11, f32[256,128]{1,0:T(8,128)} %bitcast.12, bf16[512,256]{1,0:T(8,128)(2,1)} %constant.8.clone.first_any, f32[512,128]{1,0:T(8,128)} %constant.9.clone.twist_any, bf16[64,256]{1,0:T(8,128)(2,1)} %constant.10.clone.second_any, ...), custom_call_target="tpu_custom_call" | custom-call | tf_op jit(solution)/shard_map/correlator/pallas_call | solution.py:453
  60.4 0.0 copy-start
  60.4 1.2 %copy-done = bf16[4096,128]{1,0:T(8,128)(2,1)S(1)} copy-done((bf16[4096,128]{1,0:T(8,128)(2,1)S(1)}, bf16[4096,128]{1,0:T(8,128)(2,1)}, u32[]{:S(2)}) %copy-start) | copy-done | bytes 1048600
  61.6 1.7 %turn.1 = bf16[64,64,128]{2,1,0:T(8,128)(2,1)} custom-call(bf16[4096,128]{1,0:T(8,128)(2,1)S(1)} %copy-done), custom_call_target="tpu_custom_call" | custom-call | tf_op jit(solution)/shard_map/turn/pallas_call | solution.py:482
Async XLA Ops:
  60.4 1.2 %copy-start = (bf16[4096,128]{1,0:T(8,128)(2,1)S(1)}, bf16[4096,128]{1,0:T(8,128)(2,1)}, u32[]{:S(2)}) copy-start(bf16[4096,128]{1,0:T(8,128)(2,1)} %correlator.1.vis_any) | copy-start | bytes 3145732

commit v3 on v2

--- a/solution.py
+++ b/solution.py
@@ -113,12 +113,12 @@
 
 
 def correlator_kernel(
-    dims, x_any, coef_any, first_any, twist_any, second_any, order_any, half_ref,
+    dims, x_any, coef_any, first_any, twist_any, second_any, order_any, out_any,
     x_ref, coef_in, first_ref, twist_ref, second_ref, order_ref, coef_ref,
-    real_ref, imag_ref, turn_ref, send_ref, recv_ref, line_ref, quad_ref, sum_ref, vis_ref,
+    real_ref, imag_ref, turn_ref, send_ref, recv_ref, line_ref, quad_ref, sum_ref, vis_ref, half_ref,
     load_sem, x_sem, send_sem, recv_sem, own_sem,
 ):
-    peers, in_local, nspec, taps, kept, span, step, pad = dims
+    peers, in_local, nspec, taps, kept, span, head, tail, pieces, pad = dims
     rows = first_ref.shape[1]
     width_a = rows // in_local
     parts = nspec // span
@@ -140,7 +140,6 @@
         )
         return carry
 
-    lax.fori_loop(0, peers - 1, greet, 0)
 
     def load_frames(start, count, n):
         at = pl.ds(start * rows, count * rows)
@@ -163,6 +162,7 @@
         copy.start()
     for n in range(1, parts):
         load_part(n).start()
+    lax.fori_loop(0, peers - 1, greet, 0)
 
     small[0].wait()
     for m in range(taps):
@@ -226,18 +226,25 @@
             parts_out.append(part.reshape(peers, per_dest, WIDTH_B))
         send_ref[:, h * groups + kp] = jnp.concatenate(parts_out, axis=1).astype(BF16)
 
-    def remote(c, size, n):
+    def remote(c, h, start, size, n):
         dest = partner(n)
-        at = pl.ds((c + 1) * step - size, size)
+        at = pl.ds(h * groups + start, size)
         return pltpu.make_async_remote_copy(
             src_ref=send_ref.at[dest, at], dst_ref=recv_ref.at[me, at],
             send_sem=send_sem.at[c, n], recv_sem=recv_sem.at[c, n],
             device_id={"inputs": dest}, device_id_type=pl.DeviceIdType.MESH,
         )
 
-    def push(c, size):
+    def push(c, h, start, size):
         def one(n, u):
-            remote(c, size, n).start()
+            remote(c, h, start, size, n).start()
+            return u
+
+        lax.fori_loop(0, peers - 1, one, 0)
+
+    def arrive(c, h, start, size):
+        def one(n, u):
+            remote(c, h, start, size, n).wait()
             return u
 
         lax.fori_loop(0, peers - 1, one, 0)
@@ -251,29 +258,39 @@
 
         lax.fori_loop(0, span // 2, spectra, 0, unroll=4)
 
-        @pl.when(h == 0)
+        def two_groups(n, u):
+            channel_group(h, 2 * n)
+            channel_group(h, 2 * n + 1)
+            return u
+
+        is_first = h == 0
+        is_last = h == parts - 1
+        cut = jnp.where(is_first, head // 2, jnp.where(is_last, tail // 2, 0))
+        lax.fori_loop(0, cut, two_groups, 0)
+
+        @pl.when(is_first)
         def _():
             pl.semaphore_wait(barrier, peers - 1)
-
-        def send_chunk(c, u):
-            def one(n, v):
-                channel_group(h, c * step + n)
-                return v
-
-            lax.fori_loop(0, step, one, 0, unroll=2)
-            split = (h == 0) | (h == parts - 1)
-
-            @pl.when(split)
-            def _():
-                push(2 * h + c, step)
-
-            @pl.when(jnp.logical_not(split) & (c == 1))
-            def _():
-                push(2 * h + c, groups)
-
-            return u
-
-        lax.fori_loop(0, 2, send_chunk, 0)
+            push(0, h, 0, head)
+
+        @pl.when(is_last)
+        def _():
+            push(2 * h, h, 0, tail)
+
+        lax.fori_loop(cut, groups // 2, two_groups, 0)
+
+        @pl.when(is_first)
+        def _():
+            push(1, h, head, groups - head)
+
+        @pl.when(is_last)
+        def _():
+            push(2 * h + 1, h, tail, groups - tail)
+
+        @pl.when(jnp.logical_not(is_first | is_last))
+        def _():
+            push(2 * h + 1, h, 0, groups)
+
         return carry
 
     lax.fori_loop(0, parts, forward, 0)
@@ -342,13 +359,6 @@
                 c = (s % halves) * width_a + (kp * 2 + s // halves) * shared + u
                 vis_ref[pl.ds(c, low, stride=channels), :] = vis * (1.0 / nspec)
 
-    def arrive(c, size):
-        def one(n, u):
-            remote(c, size, n).wait()
-            return u
-
-        lax.fori_loop(0, peers - 1, one, 0)
-
     def lines(h):
         def one(n, u):
             line_up(h * groups + n)
@@ -357,7 +367,7 @@
         lax.fori_loop(0, groups, one, 0, unroll=2)
 
     def middle(h, carry):
-        arrive(2 * h + 1, groups)
+        arrive(2 * h + 1, h, 0, groups)
         lines(h)
 
         @pl.when(h == parts - 3)
@@ -366,24 +376,32 @@
 
         return carry
 
-    def finish(c, carry):
-        arrive(2 * (parts - 1) + c, step)
-
-        def one(n, u):
-            kp = c * step + n
-            line_up((parts - 1) * groups + kp)
-            correlate(kp)
-            return u
-
-        lax.fori_loop(0, step, one, 0)
-        return carry
-
-    arrive(0, step)
-    arrive(1, step)
+    def finish(n, u):
+        line_up((parts - 1) * groups + n)
+        correlate(n)
+        return u
+
+    arrive(0, 0, 0, head)
+    arrive(1, 0, head, groups - head)
     lines(0)
     lax.fori_loop(1, parts - 1, middle, 0)
-    lax.fori_loop(0, 2, finish, 0)
-    half_ref[...] = vis_ref[...].astype(BF16)
+    arrive(2 * parts - 2, parts - 1, 0, tail)
+    lax.fori_loop(0, tail, finish, 0, unroll=2)
+    arrive(2 * parts - 1, parts - 1, tail, groups - tail)
+    lax.fori_loop(tail, groups, finish, 0, unroll=2)
+
+    piece = vis_ref.shape[0] // pieces
+
+    def put(p):
+        at = pl.ds(p * piece, piece)
+        return pltpu.make_async_copy(half_ref.at[at], out_any.at[at], load_sem.at[p])
+
+    for p in range(pieces):
+        at = slice(p * piece, (p + 1) * piece)
+        half_ref[at, :] = vis_ref[at, :].astype(BF16)
+        put(p).start()
+    for p in range(pieces):
+        put(p).wait()
 
 
 def turn_kernel(channels, pieces, vis_any, out_any, vis_ref, out_ref, in_sem, out_sem):
@@ -432,7 +450,8 @@
     pad = 1
     parts = nspec // span
     groups = width_a * span // WIDTH_B
-    step = groups // 2
+    head = 2
+    tail = groups // 2
     chunks = 2 * parts
     per = 2 * (kept // peers)
     count = peers * in_local
@@ -452,11 +471,11 @@
     inputs = (x, coefs, first, twist, second, order)
     vis = pl.pallas_call(
         functools.partial(
-            correlator_kernel, (peers, in_local, nspec, taps, kept, span, step, pad)
+            correlator_kernel, (peers, in_local, nspec, taps, kept, span, head, tail, pieces, pad)
         ),
         out_shape=jax.ShapeDtypeStruct((count // 2 * channels, 2 * count), BF16),
         in_specs=[pl.BlockSpec(memory_space=pl.ANY)] * len(inputs),
-        out_specs=pl.BlockSpec(memory_space=pltpu.VMEM),
+        out_specs=pl.BlockSpec(memory_space=pl.ANY),
         scratch_shapes=[pltpu.VMEM(a.shape, a.dtype) for a in inputs] + [
             pltpu.VMEM((taps * rows, WIDTH_B), F32),
             pltpu.VMEM((rows * (span + pad), WIDTH_B), F32),
@@ -468,6 +487,7 @@
             pltpu.VMEM(lines, BF16),
             pltpu.VMEM((groups * per, per * count, WIDTH_B), F32),
             pltpu.VMEM((count // 2 * channels, 2 * count), F32),
+            pltpu.VMEM((count // 2 * channels, 2 * count), BF16),
             pltpu.SemaphoreType.DMA((len(inputs) - 1,)),
             pltpu.SemaphoreType.DMA((parts + 1,)),
             pltpu.SemaphoreType.DMA((chunks, peers)),
@@ -490,7 +510,7 @@
             pltpu.SemaphoreType.DMA((pieces,)),
             pltpu.SemaphoreType.DMA((2, pieces)),
         ],
-        compiler_params=pltpu.CompilerParams(vmem_limit_bytes=32 * 2**20),
+        compiler_params=pltpu.CompilerParams(vmem_limit_bytes=60 * 2**20),
         name="turn",
     )(vis)
     return out.transpose(2, 0, 1)

time: 63.5 us -> 61.7 us (0.972)
  local copies, waits for them, and re-layouts: 1.22 us -> 0 us
    pallas_call x1, Pallas kernels: 60.3 us -> 58.9 us  [kernel_body(): pl.pallas_call(functools.partial(correlator_kernel, (peers, in_local, nsp...]
    unnamed x2 -> x0, local copies, waits for them, and re-layouts: 1.22 us -> none
    pallas_call x1, Pallas kernels: 1.74 us -> 2.62 us  [kernel_body(): pl.pallas_call(functools.partial(turn_kernel, channels, pieces), out_shap...]
where the time goes in v3:
time: 61.7 us; the launch traced here: 61.5 us
  Pallas kernels  61.5 us (100%)
    pallas_call x1, Pallas kernels, kernel_body(): pl.pallas_call(functools.partial(correlator_kernel, (peers, in_local, nsp...  58.9 us
    pallas_call x1, Pallas kernels, kernel_body(): pl.pallas_call(functools.partial(turn_kernel, channels, pieces), out_shap...  2.62 us

profile of v3, /device:TPU:0, one launch (start us, length us, event | category | flops | bytes accessed | tf_op | source)
XLA Modules:
  0.0 61.5 jit_solution(11696996869162187759)
XLA Ops:
  0.0 58.9 %correlator.1.vis_any = bf16[4096,128]{1,0:T(8,128)(2,1)} custom-call(bf16[17152,128]{1,0:T(8,128)(2,1)} %bitcast.11, f32[256,128]{1,0:T(8,128)} %bitcast.12, bf16[512,256]{1,0:T(8,128)(2,1)} %constant.8.clone.first_any, f32[512,128]{1,0:T(8,128)} %constant.9.clone.twist_any, bf16[64,256]{1,0:T(8,128)(2,1)} %constant.10.clone.second_any, ...), custom_call_target="tpu_custom_call" | custom-call | tf_op jit(solution)/shard_map/correlator/pallas_call | solution.py:472
  58.9 2.6 %turn.1 = bf16[64,64,128]{2,1,0:T(8,128)(2,1)} custom-call(bf16[4096,128]{1,0:T(8,128)(2,1)} %correlator.1.vis_any), custom_call_target="tpu_custom_call" | custom-call | tf_op jit(solution)/shard_map/turn/pallas_call | solution.py:502

commit v4 on v3

--- a/solution.py
+++ b/solution.py
@@ -404,25 +404,16 @@
         put(p).wait()
 
 
-def turn_kernel(channels, pieces, vis_any, out_any, vis_ref, out_ref, in_sem, out_sem):
+def turn_kernel(channels, pieces, vis_ref, out_any, out_ref, out_sem):
     half = out_ref.shape[0] // 2
     width = out_ref.shape[1]
     each = half // pieces
 
-    def fetch(p):
-        at = pl.ds(p * each * channels, each * channels)
-        return pltpu.make_async_copy(vis_any.at[at], vis_ref.at[at], in_sem.at[p])
-
     def put(p, upper):
         at = pl.ds(p * each + upper * half, each)
         return pltpu.make_async_copy(out_ref.at[at], out_any.at[at], out_sem.at[upper, p])
 
     for p in range(pieces):
-        fetch(p).start()
-
-    for p in range(pieces):
-        fetch(p).wait()
-
         def one_row(n, carry):
             i = p * each + n
             block = vis_ref[pl.ds(pl.multiple_of(i * channels, channels), channels), :]
@@ -431,7 +422,7 @@
             out_ref[i + half] = block[width:]
             return carry
 
-        lax.fori_loop(0, each, one_row, 0, unroll=4)
+        lax.fori_loop(0, each, one_row, 0, unroll=8)
         put(p, 0).start()
         put(p, 1).start()
     for p in range(pieces):
@@ -469,6 +460,7 @@
     blocks = (peers, parts * groups, per * in_local, WIDTH_B)
     lines = (parts * groups, per * count, WIDTH_B)
     inputs = (x, coefs, first, twist, second, order)
+    inputs = [pltpu.with_memory_space_constraint(a, pltpu.HBM) for a in inputs]
     vis = pl.pallas_call(
         functools.partial(
             correlator_kernel, (peers, in_local, nspec, taps, kept, span, head, tail, pieces, pad)
@@ -495,22 +487,20 @@
             pltpu.SemaphoreType.DMA,
         ],
         compiler_params=pltpu.CompilerParams(
-            collective_id=0, has_side_effects=True, vmem_limit_bytes=56 * 2**20
+            collective_id=0, has_side_effects=True, vmem_limit_bytes=48 * 2**20
         ),
         name="correlator",
     )(*inputs)
     out = pl.pallas_call(
         functools.partial(turn_kernel, channels, pieces),
         out_shape=jax.ShapeDtypeStruct((count, count, channels), BF16),
-        in_specs=[pl.BlockSpec(memory_space=pltpu.HBM)],
+        in_specs=[pl.BlockSpec(memory_space=pltpu.VMEM)],
         out_specs=pl.BlockSpec(memory_space=pl.ANY),
         scratch_shapes=[
-            pltpu.VMEM((count // 2 * channels, 2 * count), BF16),
             pltpu.VMEM((count, count, channels), BF16),
-            pltpu.SemaphoreType.DMA((pieces,)),
             pltpu.SemaphoreType.DMA((2, pieces)),
         ],
-        compiler_params=pltpu.CompilerParams(vmem_limit_bytes=60 * 2**20),
+        compiler_params=pltpu.CompilerParams(vmem_limit_bytes=16 * 2**20),
         name="turn",
     )(vis)
     return out.transpose(2, 0, 1)

time: 61.7 us -> 59.4 us (0.963)
  Pallas kernels: 61.5 us -> 59.3 us
    pallas_call x1, Pallas kernels: 2.62 us -> 1.17 us  [kernel_body(): pl.pallas_call(functools.partial(turn_kernel, channels, pieces), out_shap...]
    pallas_call x1, Pallas kernels: 58.9 us -> 58.1 us  [kernel_body(): pl.pallas_call(functools.partial(correlator_kernel, (peers, in_local, nsp...]
where the time goes in v4:
time: 59.4 us; the launch traced here: 59.3 us
  Pallas kernels  59.3 us (100%)
    pallas_call x1, Pallas kernels, kernel_body(): pl.pallas_call(functools.partial(correlator_kernel, (peers, in_local, nsp...  58.1 us

profile of v4, /device:TPU:0, one launch (start us, length us, event | category | flops | bytes accessed | tf_op | source)
XLA Modules:
  0.0 59.3 jit_solution(14192512664201343492)
XLA Ops:
  0.0 58.1 %correlator.1.vis_ref = bf16[4096,128]{1,0:T(8,128)(2,1)S(1)} custom-call(bf16[17152,128]{1,0:T(8,128)(2,1)} %bitcast.11, f32[256,128]{1,0:T(8,128)} %bitcast.12, bf16[512,256]{1,0:T(8,128)(2,1)} %constant.8.clone.first_any, f32[512,128]{1,0:T(8,128)} %constant.9.clone.twist_any, bf16[64,256]{1,0:T(8,128)(2,1)} %constant.10.clone.second_any, ...), custom_call_target="tpu_custom_call" | custom-call | tf_op jit(solution)/shard_map/correlator/pallas_call | solution.py:464
  58.1 1.2 %turn.1 = bf16[64,64,128]{2,1,0:T(8,128)(2,1)} custom-call(bf16[4096,128]{1,0:T(8,128)(2,1)S(1)} %correlator.1.vis_ref), custom_call_target="tpu_custom_call" | custom-call | tf_op jit(solution)/shard_map/turn/pallas_call | solution.py:494

commit v5 on v4

--- a/solution.py
+++ b/solution.py
@@ -113,9 +113,9 @@
 
 
 def correlator_kernel(
-    dims, x_any, coef_any, first_any, twist_any, second_any, order_any, out_any,
+    dims, x_any, coef_any, first_any, twist_any, second_any, order_any, vis_ref,
     x_ref, coef_in, first_ref, twist_ref, second_ref, order_ref, coef_ref,
-    real_ref, imag_ref, turn_ref, send_ref, recv_ref, line_ref, quad_ref, sum_ref, vis_ref, half_ref,
+    real_ref, imag_ref, turn_ref, send_ref, recv_ref, line_ref, quad_ref, sum_ref,
     load_sem, x_sem, send_sem, recv_sem, own_sem,
 ):
     peers, in_local, nspec, taps, kept, span, head, tail, pieces, pad = dims
@@ -265,7 +265,7 @@
 
         is_first = h == 0
         is_last = h == parts - 1
-        cut = jnp.where(is_first, head // 2, jnp.where(is_last, tail // 2, 0))
+        cut = jnp.where(is_first, head // 2, 0)
         lax.fori_loop(0, cut, two_groups, 0)
 
         @pl.when(is_first)
@@ -273,19 +273,17 @@
             pl.semaphore_wait(barrier, peers - 1)
             push(0, h, 0, head)
 
-        @pl.when(is_last)
-        def _():
-            push(2 * h, h, 0, tail)
-
-        lax.fori_loop(cut, groups // 2, two_groups, 0)
+        def piece(j, u):
+            lax.fori_loop(j * (tail // 2), (j + 1) * (tail // 2), two_groups, 0)
+            push(2 * parts - 2 + j, h, j * tail, tail)
+            return u
+
+        lax.fori_loop(0, jnp.where(is_last, groups // tail, 0), piece, 0)
+        lax.fori_loop(cut, jnp.where(is_last, 0, groups // 2), two_groups, 0)
 
         @pl.when(is_first)
         def _():
             push(1, h, head, groups - head)
-
-        @pl.when(is_last)
-        def _():
-            push(2 * h + 1, h, tail, groups - tail)
 
         @pl.when(jnp.logical_not(is_first | is_last))
         def _():
@@ -321,12 +319,14 @@
         return pltpu.roll(v, wide, 1)
 
     def line_up(g):
+        both = [recv_ref[:, g + n].reshape(per * count, WIDTH_B) for n in range(2)]
         lined = jnp.dot(
-            order_ref[...], recv_ref[:, g].reshape(per * count, WIDTH_B),
-            preferred_element_type=F32,
+            order_ref[...], jnp.concatenate(both, axis=1), preferred_element_type=F32
         )
-        line_ref[g] = lined.astype(BF16)
-        quad_ref[g] = (swap(lined) * signs).astype(BF16)
+        for n in range(2):
+            one = lined[:, n * WIDTH_B:(n + 1) * WIDTH_B]
+            line_ref[g + n] = one.astype(BF16)
+            quad_ref[g + n] = (swap(one) * signs).astype(BF16)
 
     def gram(kp, s, first, last):
         at = slice(s * count, (s + 1) * count)
@@ -361,10 +361,10 @@
 
     def lines(h):
         def one(n, u):
-            line_up(h * groups + n)
+            line_up(h * groups + 2 * n)
             return u
 
-        lax.fori_loop(0, groups, one, 0, unroll=2)
+        lax.fori_loop(0, groups // 2, one, 0)
 
     def middle(h, carry):
         arrive(2 * h + 1, h, 0, groups)
@@ -377,31 +377,21 @@
         return carry
 
     def finish(n, u):
-        line_up((parts - 1) * groups + n)
-        correlate(n)
+        line_up((parts - 1) * groups + 2 * n)
+        correlate(2 * n)
+        correlate(2 * n + 1)
+        return u
+
+    def last_part(j, u):
+        arrive(2 * parts - 2 + j, parts - 1, j * tail, tail)
+        lax.fori_loop(j * (tail // 2), (j + 1) * (tail // 2), finish, 0)
         return u
 
     arrive(0, 0, 0, head)
     arrive(1, 0, head, groups - head)
     lines(0)
     lax.fori_loop(1, parts - 1, middle, 0)
-    arrive(2 * parts - 2, parts - 1, 0, tail)
-    lax.fori_loop(0, tail, finish, 0, unroll=2)
-    arrive(2 * parts - 1, parts - 1, tail, groups - tail)
-    lax.fori_loop(tail, groups, finish, 0, unroll=2)
-
-    piece = vis_ref.shape[0] // pieces
-
-    def put(p):
-        at = pl.ds(p * piece, piece)
-        return pltpu.make_async_copy(half_ref.at[at], out_any.at[at], load_sem.at[p])
-
-    for p in range(pieces):
-        at = slice(p * piece, (p + 1) * piece)
-        half_ref[at, :] = vis_ref[at, :].astype(BF16)
-        put(p).start()
-    for p in range(pieces):
-        put(p).wait()
+    lax.fori_loop(0, groups // tail, last_part, 0)
 
 
 def turn_kernel(channels, pieces, vis_ref, out_any, out_ref, out_sem):
@@ -417,7 +407,7 @@
         def one_row(n, carry):
             i = p * each + n
             block = vis_ref[pl.ds(pl.multiple_of(i * channels, channels), channels), :]
-            block = block.astype(F32).T.astype(BF16)
+            block = block.T.astype(BF16)
             out_ref[i] = block[:width]
             out_ref[i + half] = block[width:]
             return carry
@@ -442,8 +432,8 @@
     parts = nspec // span
     groups = width_a * span // WIDTH_B
     head = 2
-    tail = groups // 2
-    chunks = 2 * parts
+    tail = 4
+    chunks = 2 * parts - 2 + groups // tail
     per = 2 * (kept // peers)
     count = peers * in_local
     channels = width_a * per // 2
@@ -465,9 +455,9 @@
         functools.partial(
             correlator_kernel, (peers, in_local, nspec, taps, kept, span, head, tail, pieces, pad)
         ),
-        out_shape=jax.ShapeDtypeStruct((count // 2 * channels, 2 * count), BF16),
+        out_shape=jax.ShapeDtypeStruct((count // 2 * channels, 2 * count), F32),
         in_specs=[pl.BlockSpec(memory_space=pl.ANY)] * len(inputs),
-        out_specs=pl.BlockSpec(memory_space=pl.ANY),
+        out_specs=pl.BlockSpec(memory_space=pltpu.VMEM),
         scratch_shapes=[pltpu.VMEM(a.shape, a.dtype) for a in inputs] + [
             pltpu.VMEM((taps * rows, WIDTH_B), F32),
             pltpu.VMEM((rows * (span + pad), WIDTH_B), F32),
@@ -478,8 +468,6 @@
             pltpu.VMEM(lines, BF16),
             pltpu.VMEM(lines, BF16),
             pltpu.VMEM((groups * per, per * count, WIDTH_B), F32),
-            pltpu.VMEM((count // 2 * channels, 2 * count), F32),
-            pltpu.VMEM((count // 2 * channels, 2 * count), BF16),
             pltpu.SemaphoreType.DMA((len(inputs) - 1,)),
             pltpu.SemaphoreType.DMA((parts + 1,)),
             pltpu.SemaphoreType.DMA((chunks, peers)),

time: 59.4 us -> 58.8 us (0.990)
  Pallas kernels: 59.3 us -> 58.6 us
    pallas_call x1, Pallas kernels: 58.1 us -> 57.5 us  [kernel_body(): pl.pallas_call(functools.partial(correlator_kernel, (peers, in_local, nsp...]
where the time goes in v5:
time: 58.8 us; the launch traced here: 58.6 us
  Pallas kernels  58.6 us (100%)
    pallas_call x1, Pallas kernels, kernel_body(): pl.pallas_call(functools.partial(correlator_kernel, (peers, in_local, nsp...  57.5 us

profile of v5, /device:TPU:0, one launch (start us, length us, event | category | flops | bytes accessed | tf_op | source)
XLA Modules:
  0.0 58.6 jit_solution(2855801244253669198)
XLA Ops:
  0.0 57.5 %correlator.1.vis_ref = f32[4096,128]{1,0:T(8,128)S(1)} custom-call(bf16[17152,128]{1,0:T(8,128)(2,1)} %bitcast.11, f32[256,128]{1,0:T(8,128)} %bitcast.12, bf16[512,256]{1,0:T(8,128)(2,1)} %constant.8.clone.first_any, f32[512,128]{1,0:T(8,128)} %constant.9.clone.twist_any, bf16[64,256]{1,0:T(8,128)(2,1)} %constant.10.clone.second_any, ...), custom_call_target="tpu_custom_call" | custom-call | tf_op jit(solution)/shard_map/correlator/pallas_call | solution.py:454
  57.5 1.2 %turn.1 = bf16[64,64,128]{2,1,0:T(8,128)(2,1)} custom-call(f32[4096,128]{1,0:T(8,128)S(1)} %correlator.1.vis_ref), custom_call_target="tpu_custom_call" | custom-call | tf_op jit(solution)/shard_map/turn/pallas_call | solution.py:482

commit v6 on v5

--- a/solution.py
+++ b/solution.py
@@ -126,6 +126,7 @@
     wide = shared * span
     groups = width_a // (2 * shared)
     slot = span + pad
+    ahead = 2
     me = lax.axis_index("inputs")
 
     def partner(n):
@@ -158,10 +159,8 @@
     small[0].start()
     load_frames(0, taps - 1, parts).start()
     load_part(0).start()
-    for copy in small[1:]:
+    for copy in small[1:-1]:
         copy.start()
-    for n in range(1, parts):
-        load_part(n).start()
     lax.fori_loop(0, peers - 1, greet, 0)
 
     small[0].wait()
@@ -169,7 +168,7 @@
         tap = coef_in[pl.ds(m, width_a, stride=taps), :]
         for i in range(in_local):
             coef_ref[pl.ds(m * rows + i, width_a, stride=in_local), :] = tap
-    for copy in small[1:]:
+    for copy in small[1:-1]:
         copy.wait()
     load_frames(0, taps - 1, parts).wait()
 
@@ -252,6 +251,10 @@
     def forward(h, carry):
         load_part(h).wait()
 
+        @pl.when(h < parts - 1)
+        def _():
+            load_part(h + 1).start()
+
         def spectra(tp, u):
             two_spectra(h, tp)
             return u
@@ -273,18 +276,29 @@
             pl.semaphore_wait(barrier, peers - 1)
             push(0, h, 0, head)
 
-        def piece(j, u):
-            lax.fori_loop(j * (tail // 2), (j + 1) * (tail // 2), two_groups, 0)
-            push(2 * parts - 2 + j, h, j * tail, tail)
-            return u
-
-        lax.fori_loop(0, jnp.where(is_last, groups // tail, 0), piece, 0)
-        lax.fori_loop(cut, jnp.where(is_last, 0, groups // 2), two_groups, 0)
+        lax.fori_loop(cut, groups // 2, two_groups, 0)
 
         @pl.when(is_first)
         def _():
             push(1, h, head, groups - head)
 
+        @pl.when(is_last)
+        def _():
+            def piece(q, u):
+                later = q // (groups // tail)
+                j = q % (groups // tail)
+
+                def one(n, v):
+                    @pl.when((partner(n) >= ahead) == (later == 1))
+                    def _():
+                        remote(2 * parts - 2 + j, h, j * tail, tail, n).start()
+
+                    return v
+
+                return lax.fori_loop(0, peers - 1, one, u)
+
+            lax.fori_loop(0, 2 * (groups // tail), piece, 0)
+
         @pl.when(jnp.logical_not(is_first | is_last))
         def _():
             push(2 * h + 1, h, 0, groups)
@@ -292,6 +306,8 @@
         return carry
 
     lax.fori_loop(0, parts, forward, 0)
+    small[-1].start()
+    small[-1].wait()
     own = pltpu.make_async_copy(send_ref.at[me], recv_ref.at[me], own_sem)
     own.start()
     own.wait()
@@ -372,7 +388,7 @@
 
         @pl.when(h == parts - 3)
         def _():
-            lax.fori_loop(0, groups, correlate_early, 0)
+            lax.fori_loop(0, groups, correlate_early, 0, unroll=2)
 
         return carry
 
@@ -384,7 +400,8 @@
 
     def last_part(j, u):
         arrive(2 * parts - 2 + j, parts - 1, j * tail, tail)
-        lax.fori_loop(j * (tail // 2), (j + 1) * (tail // 2), finish, 0)
+        for n in range(tail // 2):
+            finish(j * (tail // 2) + n, 0)
         return u
 
     arrive(0, 0, 0, head)

time: 58.8 us -> 57.4 us (0.976)
  Pallas kernels: 58.6 us -> 57.2 us
    pallas_call x1, Pallas kernels: 57.5 us -> 56 us  [kernel_body(): pl.pallas_call(functools.partial(correlator_kernel, (peers, in_local, nsp...]
where the time goes in v6:
time: 57.4 us; the launch traced here: 57.2 us
  Pallas kernels  57.2 us (100%)
    pallas_call x1, Pallas kernels, kernel_body(): pl.pallas_call(functools.partial(correlator_kernel, (peers, in_local, nsp...  56 us
    pallas_call x1, Pallas kernels, kernel_body(): pl.pallas_call(functools.partial(turn_kernel, channels, pieces), out_shap...  1.17 us

profile of v6, /device:TPU:0, one launch (start us, length us, event | category | flops | bytes accessed | tf_op | source)
XLA Modules:
  0.0 57.2 jit_solution(6497812696915124641)
XLA Ops:
  0.0 56.0 %correlator.1.vis_ref = f32[4096,128]{1,0:T(8,128)S(1)} custom-call(bf16[17152,128]{1,0:T(8,128)(2,1)} %bitcast.11, f32[256,128]{1,0:T(8,128)} %bitcast.12, bf16[512,256]{1,0:T(8,128)(2,1)} %constant.8.clone.first_any, f32[512,128]{1,0:T(8,128)} %constant.9.clone.twist_any, bf16[64,256]{1,0:T(8,128)(2,1)} %constant.10.clone.second_any, ...), custom_call_target="tpu_custom_call" | custom-call | tf_op jit(solution)/shard_map/correlator/pallas_call | solution.py:471
  56.0 1.2 %turn.1 = bf16[64,64,128]{2,1,0:T(8,128)(2,1)} custom-call(f32[4096,128]{1,0:T(8,128)S(1)} %correlator.1.vis_ref), custom_call_target="tpu_custom_call" | custom-call | tf_op jit(solution)/shard_map/turn/pallas_call | solution.py:499

commit v7 on v6

--- a/solution.py
+++ b/solution.py
@@ -100,10 +100,14 @@
 
 def make_tables(in_local, width_a, kept):
     nfft = width_a * WIDTH_B
-    first = np.concatenate([t.T for t in np_phase(width_a, width_a, width_a)], axis=0)
+    half = width_a // 2
+    cos_a, sin_a = (t.T for t in np_phase(width_a, width_a, width_a))
+    first = np.concatenate([cos_a[:half + 1], sin_a[1:half]], axis=0)
     first = np.kron(first, np.eye(in_local, dtype=np.float32))
+    mirrored = [*range(half + 1), *range(width_a - 1, half, -1)]
     twist = np.concatenate(
-        [np.repeat(t, in_local, axis=0) for t in np_phase(width_a, WIDTH_B, nfft)], axis=0
+        [np.repeat(t[mirrored], in_local, axis=0) for t in np_phase(width_a, WIDTH_B, nfft)],
+        axis=0,
     )
     cos_b, sin_b = (t[:, :kept].T for t in np_phase(WIDTH_B, WIDTH_B, WIDTH_B))
     second = np.concatenate(
@@ -125,7 +129,7 @@
     shared = WIDTH_B // (2 * span)
     wide = shared * span
     groups = width_a // (2 * shared)
-    slot = span + pad
+    slot = rows + pad
     ahead = 2
     me = lax.axis_index("inputs")
 
@@ -173,6 +177,8 @@
     load_frames(0, taps - 1, parts).wait()
 
     lane_block = 64
+    low_rows = rows // 2
+    edge = lax.broadcasted_iota(jnp.int32, (8, WIDTH_B), 0) < in_local
 
     def two_spectra(h, tp):
         late_t = tp * 2
@@ -194,12 +200,19 @@
             filtered.append(jnp.concatenate(pair, axis=1))
         filtered = jnp.concatenate(filtered, axis=0)
         out = jnp.dot(first_ref[...], filtered, preferred_element_type=F32)
-        w_re, w_im = twist_ref[:rows, :], twist_ref[rows:, :]
+        w_re, w_im = twist_ref[:low_rows, :], twist_ref[rows:rows + low_rows, :]
+        v_re, v_im = twist_ref[low_rows:rows, :], twist_ref[rows + low_rows:, :]
         for late in range(2):
             cols = slice(late * WIDTH_B, (late + 1) * WIDTH_B)
-            re, im = out[:rows, cols], out[rows:, cols]
-            real_ref[pl.ds(late_t + late, rows, stride=slot), :] = re * w_re - im * w_im
-            imag_ref[pl.ds(late_t + late, rows, stride=slot), :] = re * w_im + im * w_re
+            re, im = out[:low_rows, cols], out[low_rows:, cols]
+            mirror = jnp.concatenate([jnp.where(edge, im[:8], re[:8]), re[8:]], axis=0)
+            im = jnp.concatenate([jnp.where(edge, 0.0, im[:8]), im[8:]], axis=0)
+            at = pl.ds(pl.multiple_of((late_t + late) * slot, 8), low_rows)
+            real_ref[at, :] = re * w_re - im * w_im
+            imag_ref[at, :] = re * w_im + im * w_re
+            at = pl.ds(pl.multiple_of((late_t + late) * slot + low_rows, 8), low_rows)
+            real_ref[at, :] = mirror * v_re + im * v_im
+            imag_ref[at, :] = mirror * v_im - im * v_re
 
     per_dest = kept // peers * in_local
 
@@ -210,7 +223,8 @@
             for i in range(in_local):
                 for u in range(shared):
                     k = (kp * 2 + kk) * shared + u
-                    at = pl.ds((k * in_local + i) * slot, span)
+                    k = jnp.where(k <= width_a // 2, k, width_a // 2 * 3 - k)
+                    at = pl.ds(k * in_local + i, span, stride=slot)
                     both.append(jnp.concatenate(
                         [real_ref[at, :].astype(BF16), imag_ref[at, :].astype(BF16)], axis=1
                     ))
@@ -259,7 +273,7 @@
             two_spectra(h, tp)
             return u
 
-        lax.fori_loop(0, span // 2, spectra, 0, unroll=4)
+        lax.fori_loop(0, span // 2, spectra, 0, unroll=8)
 
         def two_groups(n, u):
             channel_group(h, 2 * n)
@@ -445,7 +459,7 @@
     rows = width_a * in_local
     span = 16
     pieces = 4
-    pad = 1
+    pad = 8
     parts = nspec // span
     groups = width_a * span // WIDTH_B
     head = 2
@@ -477,8 +491,8 @@
         out_specs=pl.BlockSpec(memory_space=pltpu.VMEM),
         scratch_shapes=[pltpu.VMEM(a.shape, a.dtype) for a in inputs] + [
             pltpu.VMEM((taps * rows, WIDTH_B), F32),
-            pltpu.VMEM((rows * (span + pad), WIDTH_B), F32),
-            pltpu.VMEM((rows * (span + pad), WIDTH_B), F32),
+            pltpu.VMEM((span * (rows + pad), WIDTH_B), F32),
+            pltpu.VMEM((span * (rows + pad), WIDTH_B), F32),
             pltpu.VMEM((2 * kept * in_local, WIDTH_B), F32),
             pltpu.VMEM(blocks, BF16),
             pltpu.VMEM(blocks, BF16),
@@ -519,7 +533,7 @@
         kept = WIDTH_B // 4
         nfft = filter_coefs.shape[1]
         nspec = samples.shape[1] // nfft - filter_coefs.shape[0] + 1
-        fits = kept % peers == 0 and 2 * peers * in_local == WIDTH_B
+        fits = kept % peers == 0 and in_local <= 8 and 2 * peers * in_local == WIDTH_B
         fits = fits and nspec % 16 == 0 and nspec >= 64 and nfft % (32 * WIDTH_B) == 0
         if fits and (2 * in_local * (kept // peers)) % 16 == 0:
             return kernel_body(peers, kept, samples, filter_coefs)

time: 57.4 us -> 57.2 us (level)
  no operation moved by 1% of the time
where the time goes in v7:
time: 57.2 us; the launch traced here: 57 us
  Pallas kernels  57 us (100%)
    pallas_call x1, Pallas kernels, kernel_body(): pl.pallas_call(functools.partial(correlator_kernel, (peers, in_local, nsp...  55.9 us
    pallas_call x1, Pallas kernels, kernel_body(): pl.pallas_call(functools.partial(turn_kernel, channels, pieces), out_shap...  1.17 us

profile of v7, /device:TPU:0, one launch (start us, length us, event | category | flops | bytes accessed | tf_op | source)
XLA Modules:
  0.0 57.0 jit_solution(17477136279404845523)
XLA Ops:
  0.0 55.9 %correlator.1.vis_ref = f32[4096,128]{1,0:T(8,128)S(1)} custom-call(bf16[17152,128]{1,0:T(8,128)(2,1)} %bitcast.11, f32[256,128]{1,0:T(8,128)} %bitcast.12, bf16[256,256]{1,0:T(8,128)(2,1)} %constant.8.clone.first_any, f32[512,128]{1,0:T(8,128)} %constant.9.clone.twist_any, bf16[64,256]{1,0:T(8,128)(2,1)} %constant.10.clone.second_any, ...), custom_call_target="tpu_custom_call" | custom-call | tf_op jit(solution)/shard_map/correlator/pallas_call | solution.py:485
  55.9 1.2 %turn.1 = bf16[64,64,128]{2,1,0:T(8,128)(2,1)} custom-call(f32[4096,128]{1,0:T(8,128)S(1)} %correlator.1.vis_ref), custom_call_target="tpu_custom_call" | custom-call | tf_op jit(solution)/shard_map/turn/pallas_call | solution.py:513

commit v8 on v7

--- a/solution.py
+++ b/solution.py
@@ -165,7 +165,7 @@
     load_part(0).start()
     for copy in small[1:-1]:
         copy.start()
-    lax.fori_loop(0, peers - 1, greet, 0)
+    lax.fori_loop(0, peers - 1, greet, 0, unroll=5)
 
     small[0].wait()
     for m in range(taps):
@@ -253,14 +253,14 @@
             remote(c, h, start, size, n).start()
             return u
 
-        lax.fori_loop(0, peers - 1, one, 0)
+        lax.fori_loop(0, peers - 1, one, 0, unroll=5)
 
     def arrive(c, h, start, size):
         def one(n, u):
             remote(c, h, start, size, n).wait()
             return u
 
-        lax.fori_loop(0, peers - 1, one, 0)
+        lax.fori_loop(0, peers - 1, one, 0, unroll=5)
 
     def forward(h, carry):
         load_part(h).wait()
@@ -370,22 +370,27 @@
         )
         return lax.dot_general(left, right, NT, preferred_element_type=F32)
 
-    def correlate_early(kp, u):
+    def select(res, u):
+        top = res[u * count:u * count + low]
+        bottom = res[u * count + low:(u + 1) * count]
+        return jnp.where(
+            first_half,
+            jnp.where(top_real, top, swap(top)),
+            jnp.where(low_real, swap(bottom), bottom),
+        )
+
+    def correlate_early(kp, carry):
         for s in range(per):
-            sum_ref[kp * per + s] = gram(kp, s, 0, parts - 2)
-        return u
+            res = gram(kp, s, 0, parts - 2)
+            for u in range(shared):
+                sum_ref[kp * per + s, u * low:(u + 1) * low, :] = select(res, u)
+        return carry
 
     def correlate(kp):
         for s in range(per):
-            res = sum_ref[kp * per + s] + gram(kp, s, parts - 2, parts)
+            res = gram(kp, s, parts - 2, parts)
             for u in range(shared):
-                top = res[u * count:u * count + low]
-                bottom = res[u * count + low:(u + 1) * count]
-                vis = jnp.where(
-                    first_half,
-                    jnp.where(top_real, top, swap(top)),
-                    jnp.where(low_real, swap(bottom), bottom),
-                )
+                vis = select(res, u) + sum_ref[kp * per + s, u * low:(u + 1) * low, :]
                 c = (s % halves) * width_a + (kp * 2 + s // halves) * shared + u
                 vis_ref[pl.ds(c, low, stride=channels), :] = vis * (1.0 / nspec)
 
@@ -498,7 +503,7 @@
             pltpu.VMEM(blocks, BF16),
             pltpu.VMEM(lines, BF16),
             pltpu.VMEM(lines, BF16),
-            pltpu.VMEM((groups * per, per * count, WIDTH_B), F32),
+            pltpu.VMEM((groups * per, WIDTH_B // (2 * span) * (count // 2), WIDTH_B), F32),
             pltpu.SemaphoreType.DMA((len(inputs) - 1,)),
             pltpu.SemaphoreType.DMA((parts + 1,)),
             pltpu.SemaphoreType.DMA((chunks, peers)),

time: 57.2 us -> 57 us (level)
  no operation moved by 1% of the time
where the time goes in v8:
time: 57 us; the launch traced here: 56.8 us
  Pallas kernels  56.8 us (100%)
    pallas_call x1, Pallas kernels, kernel_body(): pl.pallas_call(functools.partial(correlator_kernel, (peers, in_local, nsp...  55.6 us
    pallas_call x1, Pallas kernels, kernel_body(): pl.pallas_call(functools.partial(turn_kernel, channels, pieces), out_shap...  1.17 us

profile of v8, /device:TPU:0, one launch (start us, length us, event | category | flops | bytes accessed | tf_op | source)
XLA Modules:
  0.0 56.8 jit_solution(8788476193072043993)
XLA Ops:
  0.0 55.6 %correlator.1.vis_ref = f32[4096,128]{1,0:T(8,128)S(1)} custom-call(bf16[17152,128]{1,0:T(8,128)(2,1)} %bitcast.11, f32[256,128]{1,0:T(8,128)} %bitcast.12, bf16[256,256]{1,0:T(8,128)(2,1)} %constant.8.clone.first_any, f32[512,128]{1,0:T(8,128)} %constant.9.clone.twist_any, bf16[64,256]{1,0:T(8,128)(2,1)} %constant.10.clone.second_any, ...), custom_call_target="tpu_custom_call" | custom-call | tf_op jit(solution)/shard_map/correlator/pallas_call | solution.py:490
  55.6 1.2 %turn.1 = bf16[64,64,128]{2,1,0:T(8,128)(2,1)} custom-call(f32[4096,128]{1,0:T(8,128)S(1)} %correlator.1.vis_ref), custom_call_target="tpu_custom_call" | custom-call | tf_op jit(solution)/shard_map/turn/pallas_call | solution.py:518

commit v9 on v8

--- a/solution.py
+++ b/solution.py
@@ -386,9 +386,34 @@
                 sum_ref[kp * per + s, u * low:(u + 1) * low, :] = select(res, u)
         return carry
 
+    def gram_pair(kp, s, h):
+        g = h * groups + kp
+        ats = [slice(n * count, (n + 1) * count) for n in (s, s + 1)]
+        tiles = [line_ref[g, at, :] for at in ats]
+        sides = [jnp.concatenate([line_ref[g, at, :], quad_ref[g, at, :]], axis=0) for at in ats]
+        none = jnp.zeros_like(sides[0])
+        right = jnp.concatenate([
+            jnp.concatenate([sides[0], none], axis=1), jnp.concatenate([none, sides[1]], axis=1)
+        ], axis=0)
+        left = jnp.concatenate(
+            [jnp.concatenate([t * m for t in tiles], axis=1) for m in masks], axis=0
+        )
+        return lax.dot_general(left, right, NT, preferred_element_type=F32)
+
+    def correlate_more(kp, carry):
+        for s in range(per):
+            if s % 2 == 0:
+                both = gram_pair(kp, s, parts - 2)
+            res = both[:, s % 2 * WIDTH_B:(s % 2 + 1) * WIDTH_B]
+            for u in range(shared):
+                sum_ref[kp * per + s, u * low:(u + 1) * low, :] += select(res, u)
+        return carry
+
     def correlate(kp):
         for s in range(per):
-            res = gram(kp, s, parts - 2, parts)
+            if s % 2 == 0:
+                both = gram_pair(kp, s, parts - 1)
+            res = both[:, s % 2 * WIDTH_B:(s % 2 + 1) * WIDTH_B]
             for u in range(shared):
                 vis = select(res, u) + sum_ref[kp * per + s, u * low:(u + 1) * low, :]
                 c = (s % halves) * width_a + (kp * 2 + s // halves) * shared + u
@@ -427,6 +452,7 @@
     arrive(1, 0, head, groups - head)
     lines(0)
     lax.fori_loop(1, parts - 1, middle, 0)
+    lax.fori_loop(0, groups, correlate_more, 0, unroll=2)
     lax.fori_loop(0, groups // tail, last_part, 0)
 
 

time: 57 us -> 57 us (level)
  no operation moved by 1% of the time
where the time goes in v9:
time: 57 us; the launch traced here: 56.9 us
  Pallas kernels  56.9 us (100%)
    pallas_call x1, Pallas kernels, kernel_body(): pl.pallas_call(functools.partial(correlator_kernel, (peers, in_local, nsp...  55.7 us
    pallas_call x1, Pallas kernels, kernel_body(): pl.pallas_call(functools.partial(turn_kernel, channels, pieces), out_shap...  1.17 us

profile of v9, /device:TPU:0, one launch (start us, length us, event | category | flops | bytes accessed | tf_op | source)
XLA Modules:
  0.0 56.9 jit_solution(465939717934368951)
XLA Ops:
  0.0 55.7 %correlator.1.vis_ref = f32[4096,128]{1,0:T(8,128)S(1)} custom-call(bf16[17152,128]{1,0:T(8,128)(2,1)} %bitcast.11, f32[256,128]{1,0:T(8,128)} %bitcast.12, bf16[256,256]{1,0:T(8,128)(2,1)} %constant.8.clone.first_any, f32[512,128]{1,0:T(8,128)} %constant.9.clone.twist_any, bf16[64,256]{1,0:T(8,128)(2,1)} %constant.10.clone.second_any, ...), custom_call_target="tpu_custom_call" | custom-call | tf_op jit(solution)/shard_map/correlator/pallas_call | solution.py:516
  55.7 1.2 %turn.1 = bf16[64,64,128]{2,1,0:T(8,128)(2,1)} custom-call(f32[4096,128]{1,0:T(8,128)S(1)} %correlator.1.vis_ref), custom_call_target="tpu_custom_call" | custom-call | tf_op jit(solution)/shard_map/turn/pallas_call | solution.py:544

commit v10 on v8

--- a/solution.py
+++ b/solution.py
@@ -150,8 +150,10 @@
         at = pl.ds(start * rows, count * rows)
         return pltpu.make_async_copy(x_any.at[at], x_ref.at[at], x_sem.at[n])
 
-    def load_part(h):
-        return load_frames(h * span + taps - 1, span, h)
+    each = span // 2
+
+    def load_part(g):
+        return load_frames(g * each + taps - 1, each, g)
 
     small = [
         pltpu.make_async_copy(src, dst, load_sem.at[n])
@@ -161,8 +163,9 @@
         ))
     ]
     small[0].start()
-    load_frames(0, taps - 1, parts).start()
+    load_frames(0, taps - 1, 2 * parts).start()
     load_part(0).start()
+    load_part(1).start()
     for copy in small[1:-1]:
         copy.start()
     lax.fori_loop(0, peers - 1, greet, 0, unroll=5)
@@ -174,7 +177,7 @@
             coef_ref[pl.ds(m * rows + i, width_a, stride=in_local), :] = tap
     for copy in small[1:-1]:
         copy.wait()
-    load_frames(0, taps - 1, parts).wait()
+    load_frames(0, taps - 1, 2 * parts).wait()
 
     lane_block = 64
     low_rows = rows // 2
@@ -263,17 +266,20 @@
         lax.fori_loop(0, peers - 1, one, 0, unroll=5)
 
     def forward(h, carry):
-        load_part(h).wait()
-
-        @pl.when(h < parts - 1)
-        def _():
-            load_part(h + 1).start()
-
         def spectra(tp, u):
             two_spectra(h, tp)
             return u
 
-        lax.fori_loop(0, span // 2, spectra, 0, unroll=8)
+        def stretch(n, u):
+            load_part(2 * h + n).wait()
+
+            @pl.when(h < parts - 1)
+            def _():
+                load_part(2 * h + 2 + n).start()
+
+            return lax.fori_loop(0, each // 2, lambda tp, v: spectra(n * (each // 2) + tp, v), u, unroll=4)
+
+        lax.fori_loop(0, 2, stretch, 0)
 
         def two_groups(n, u):
             channel_group(h, 2 * n)
@@ -505,7 +511,7 @@
             pltpu.VMEM(lines, BF16),
             pltpu.VMEM((groups * per, WIDTH_B // (2 * span) * (count // 2), WIDTH_B), F32),
             pltpu.SemaphoreType.DMA((len(inputs) - 1,)),
-            pltpu.SemaphoreType.DMA((parts + 1,)),
+            pltpu.SemaphoreType.DMA((2 * parts + 1,)),
             pltpu.SemaphoreType.DMA((chunks, peers)),
             pltpu.SemaphoreType.DMA((chunks, peers)),
             pltpu.SemaphoreType.DMA,

time: 57 us -> 57 us (level)
  no operation moved by 1% of the time
where the time goes in v10:
time: 57 us; the launch traced here: 56.8 us
  Pallas kernels  56.8 us (100%)
    pallas_call x1, Pallas kernels, kernel_body(): pl.pallas_call(functools.partial(correlator_kernel, (peers, in_local, nsp...  55.6 us
    pallas_call x1, Pallas kernels, kernel_body(): pl.pallas_call(functools.partial(turn_kernel, channels, pieces), out_shap...  1.17 us

profile of v10, /device:TPU:0, one launch (start us, length us, event | category | flops | bytes accessed | tf_op | source)
XLA Modules:
  0.0 56.8 jit_solution(6041073145569686170)
XLA Ops:
  0.0 55.6 %correlator.1.vis_ref = f32[4096,128]{1,0:T(8,128)S(1)} custom-call(bf16[17152,128]{1,0:T(8,128)(2,1)} %bitcast.11, f32[256,128]{1,0:T(8,128)} %bitcast.12, bf16[256,256]{1,0:T(8,128)(2,1)} %constant.8.clone.first_any, f32[512,128]{1,0:T(8,128)} %constant.9.clone.twist_any, bf16[64,256]{1,0:T(8,128)(2,1)} %constant.10.clone.second_any, ...), custom_call_target="tpu_custom_call" | custom-call | tf_op jit(solution)/shard_map/correlator/pallas_call | solution.py:496
  55.6 1.2 %turn.1 = bf16[64,64,128]{2,1,0:T(8,128)(2,1)} custom-call(f32[4096,128]{1,0:T(8,128)S(1)} %correlator.1.vis_ref), custom_call_target="tpu_custom_call" | custom-call | tf_op jit(solution)/shard_map/turn/pallas_call | solution.py:524
